TPU v7x, 256 devices: a whole 4x4x8 slice. The times are simulated.
256 devices in a mesh: seq: 64 (over x, z_lo, y, core), cfg: 4 (over z_hi).
Axes of the slice: x: 4, y: 4, z: 8 (z_hi: 4, z_lo: 2; z = z_hi * 2 + z_lo), core: 2. Of those that a mesh axis runs over, the one named last changes fastest.
Arguments:
- hidden: bfloat16 [131072, 1024], P(('seq', 'cfg')), may hold values from -6 to 6
- latent: float32 [80, 65536], P(None, 'seq'), may hold values from -6 to 6
- prompt_mel: float32 [80, 65536], P(None, 'seq'), may hold values from -6 to 6
- window_back: int32 [2048], P('seq'), may hold values from 0 to 4, as said below
- window_ahead: int32 [2048], P('seq'), may hold values from 0 to 4, as said below
- step_index: int32 [1], replicated, may hold values from 8 to 31
- proj_weight: bfloat16 [1024, 80], replicated, may hold values from -0.1875 to 0.1875
- latent_weight: bfloat16 [80, 1024], replicated, may hold values from -0.625 to 0.625
- prompt_weight: bfloat16 [80, 1024], replicated, may hold values from -0.625 to 0.625
- time_weight: bfloat16 [256, 3072], replicated, may hold values from -0.375 to 0.375
- qkv_weight: bfloat16 [1024, 3072], replicated
- attn_out_weight: bfloat16 [1024, 1024], replicated, may hold values from -0.1875 to 0.1875
Outputs:
- latent_next: float32 [80, 65536], P(None, ('seq', 'cfg'))
- hidden_next: bfloat16 [131072, 1024], P(('seq', 'cfg'))
Inputs may be any that keep to these rules, and one draw needn't show every extreme that they name: `window_back`: lookback of each block, in blocks of 32 frames; some block takes 4. `window_ahead`: advance of each block, in blocks of 32 frames; some block takes 4.
All inputs are finite; a program needn't handle non-finite values.
Results may differ from a plain program's by a relative error of at most 0.0065.
Values may be sent and summed in bfloat16 or wider, within the bound.
No kernel may reach another device: no remote copies, remote signals or barrier semaphores. Data moves between devices by JAX's collectives and lax.ppermute only.
A program may use at most 64 MiB of HBM per device.

v0:
```python
import math

import jax
import jax.numpy as jnp
from jax import lax
from jax.sharding import PartitionSpec as P

HEADS = 16
BLK = 32
NSTEPS = 32
HALO = 128


EPS = 1e-06
GUIDE = 0.5


def from_partner(shard, axis, distance):
    return lax.ppermute(shard, axis, [(i, i ^ 1 << distance) for i in range(lax.axis_size(axis))])


def padded(cells, sides, width):
    for axis, dim in sides:
        count = lax.axis_size(axis)
        ends = count - 1
        head = lax.slice_in_dim(cells, 0, width, axis=dim)
        tail = lax.slice_in_dim(cells, cells.shape[dim] - width, cells.shape[dim], axis=dim)
        cells = jnp.concatenate(
            [
                lax.ppermute(tail, axis, [(i, (i + 1) % count) for i in range(ends)]),
                cells,
                lax.ppermute(head, axis, [((i + 1) % count, i) for i in range(ends)]),
            ],
            axis=dim,
        )
    return cells


def layer_norm(rows):
    mean = jnp.mean(rows, axis=-1, keepdims=True)
    centered = rows - mean
    spread = jnp.mean(centered * centered, axis=-1, keepdims=True)
    return centered * lax.rsqrt(spread + EPS)


def time_value(step):
    return 1.0 - jnp.cos(0.5 * math.pi * step.astype(jnp.float32) / NSTEPS)


def modulation(step_index, time_weight):
    later = time_value(step_index[0] + 1)
    half_freq = time_weight.shape[0] // 2
    freqs = jnp.exp(-math.log(10000.0) * jnp.arange(half_freq, dtype=jnp.float32) / half_freq)
    angles = 1000.0 * later * freqs
    features = jnp.concatenate([jnp.sin(angles), jnp.cos(angles)])
    mixed = jnp.dot(
        features[None, :], time_weight.astype(jnp.float32), precision=lax.Precision.HIGHEST
    )[0]
    width = mixed.shape[0] // 3
    return (mixed[:width], mixed[width : 2 * width], mixed[2 * width :])


def embed_rows(latent_cols, prompt_cols, flag, latent_weight, prompt_weight):
    dims = (((0,), (0,)), ((), ()))
    base = lax.dot_general(
        latent_cols, latent_weight.astype(jnp.float32), dims, precision=lax.Precision.HIGHEST
    )
    extra = lax.dot_general(
        prompt_cols, prompt_weight.astype(jnp.float32), dims, precision=lax.Precision.HIGHEST
    )
    return base + flag * extra


def attention_input(first, shift, scale, qkv_weight):
    normed = (layer_norm(first) * (1.0 + scale) + shift).astype(jnp.bfloat16)
    return jnp.dot(normed, qkv_weight, preferred_element_type=jnp.float32).astype(jnp.bfloat16)


def window_mask(query_start, key_start, rows, key_count, back, ahead, frames, block):
    query_pos = query_start + jnp.arange(rows, dtype=jnp.int32)
    key_pos = key_start + jnp.arange(key_count, dtype=jnp.int32)
    query_block = query_pos // block
    key_block = key_pos // block
    back_rows = jnp.repeat(back, block, total_repeat_length=rows)
    ahead_rows = jnp.repeat(ahead, block, total_repeat_length=rows)
    lower = (query_block - back_rows)[:, None]
    upper = (query_block + ahead_rows)[:, None]
    inside = (key_pos >= 0) & (key_pos < frames)
    return (key_block[None, :] >= lower) & (key_block[None, :] <= upper) & inside[None, :]


def window_attention(query, keys, values, allowed, heads):
    rows, width = query.shape
    size = width // heads
    query_heads = query.reshape(rows, heads, size).transpose(1, 0, 2)
    key_heads = keys.reshape(-1, heads, size).transpose(1, 0, 2)
    value_heads = values.reshape(-1, heads, size).transpose(1, 0, 2)

    def one_head(operands):
        query_one, key_one, value_one = operands
        scores = jnp.dot(query_one, key_one.T, preferred_element_type=jnp.float32) / math.sqrt(size)
        scores = jnp.where(allowed, scores, -1e30)
        top = jnp.max(scores, axis=-1, keepdims=True)
        weights = jnp.exp(scores - top)
        total = jnp.sum(weights, axis=-1, keepdims=True)
        probs = (weights / total).astype(jnp.bfloat16)
        return jnp.dot(probs, value_one, preferred_element_type=jnp.float32).astype(jnp.bfloat16)

    context = lax.map(one_head, (query_heads, key_heads, value_heads))
    return context.transpose(1, 0, 2).reshape(rows, width)


def body(
    hidden,
    latent,
    prompt_mel,
    window_back,
    window_ahead,
    step_index,
    proj_weight,
    latent_weight,
    prompt_weight,
    time_weight,
    qkv_weight,
    attn_out_weight,
):
    rows, width = hidden.shape
    place = lax.axis_index("cfg")
    branch = place % 2
    half = place // 2
    seq_place = lax.axis_index("seq")
    frames = 2 * rows * lax.axis_size("seq")
    per_half = rows // BLK
    share = rows // 2
    normed = layer_norm(hidden.astype(jnp.float32)).astype(jnp.bfloat16)
    velocity = lax.dot_general(
        proj_weight, normed, (((0,), (1,)), ((), ())), preferred_element_type=jnp.float32
    )
    delta = time_value(step_index[0] + 1) - time_value(step_index[0])
    partner = from_partner(velocity, "cfg", 0)
    cond_vel = jnp.where(branch == 0, velocity, partner)
    free_vel = jnp.where(branch == 0, partner, velocity)
    own_latent = lax.dynamic_slice_in_dim(latent, half * rows, rows, 1)
    updated = own_latent + delta * (cond_vel + GUIDE * (cond_vel - free_vel))
    latent_out = lax.dynamic_slice_in_dim(updated, branch * share, share, 1)
    shift, scale, gate = modulation(step_index, time_weight)
    flag = (branch == 0).astype(jnp.float32)
    own_prompt = lax.dynamic_slice_in_dim(prompt_mel, half * rows, rows, 1)
    own_first = embed_rows(updated, own_prompt, flag, latent_weight, prompt_weight)
    packed = attention_input(own_first, shift, scale, qkv_weight)
    query = packed[:, :width]
    paired = packed[:, width:]
    edges = jnp.concatenate([paired[:HALO], paired[rows - HALO :]], 0)
    across = from_partner(edges, "cfg", 1)
    bordered = padded(across, (("seq", 0),), HALO)
    before = jnp.where(half == 1, bordered[2 * HALO : 3 * HALO], bordered[:HALO])
    after = jnp.where(half == 0, bordered[HALO : 2 * HALO], bordered[3 * HALO :])
    window = jnp.concatenate([before, paired, after], 0)
    query_start = (2 * seq_place + half) * rows
    back = lax.dynamic_slice_in_dim(window_back, half * per_half, per_half, 0)
    ahead = lax.dynamic_slice_in_dim(window_ahead, half * per_half, per_half, 0)
    allowed = window_mask(
        query_start, query_start - HALO, rows, rows + 2 * HALO, back, ahead, frames, BLK
    )
    context = window_attention(query, window[:, :width], window[:, width:], allowed, HEADS)
    projected = jnp.dot(context, attn_out_weight, preferred_element_type=jnp.float32)
    hidden_next = (own_first + gate * projected).astype(jnp.bfloat16)
    return (latent_out, hidden_next)


def solution(mesh):
    in_specs = (
        P(("seq", "cfg"), None),
        P(None, "seq"),
        P(None, "seq"),
        P("seq"),
        P("seq"),
        P(),
        P(),
        P(),
        P(),
        P(),
        P(),
        P(),
    )
    out_specs = (P(None, ("seq", "cfg")), P(("seq", "cfg"), None))
    return jax.shard_map(body, mesh=mesh, in_specs=in_specs, out_specs=out_specs, check_vma=False)
```

profile of v0, /device:TPU:6, one launch (start us, length us, event | category | flops | bytes accessed | tf_op | source)
XLA Modules:
  0.0 181.0 jit_solution(16884246420031972859)
XLA Ops:
  0.7 1.6 convert_reduce_fusion
  2.3 1.6 fusion.15
  4.0 0.6 convolution_bitcast_fusion
  4.5 3.4 %collective-permute-start = (f32[80,512]{1,0:T(8,128)S(1)}, f32[80,512]{1,0:T(8,128)S(1)}, u32[]{:S(2)}, u32[]{:S(2)}) collective-permute-start(f32[80,512]{1,0:T(8,128)S(1)} %convolution_bitcast_fusion), channel_id=1, source_target_pairs={{0,1},{1,0},{2,3},{3,2},{4,5},{5,4},{6,7},{7,6},{8,9},{9,8},{10,11... | collective-permute-start | bytes 491528 | tf_op jit(solution)/shard_map/ppermute | solution.py:19
  8.8 2.2 %fusion.46 = f32[1,3072]{1,0:T(1,128)S(1)} fusion(f32[256,1]{0,1:T(1,128)S(1)} %bitcast.189, bf16[256,3072]{1,0:T(8,128)(2,1)} %param.29), kind=kOutput, calls=%fused_computation.101 | convolution fusion | flops 9437184 | bytes 1586176 | tf_op jit(solution)/shard_map/dot_general | solution.py:56
  11.0 1.0 fusion.24
  12.0 3.6 %collective-permute-done = f32[80,512]{1,0:T(8,128)S(1)} collective-permute-done((f32[80,512]{1,0:T(8,128)S(1)}, f32[80,512]{1,0:T(8,128)S(1)}, u32[]{:S(2)}, u32[]{:S(2)}) %collective-permute-start) | collective-permute-done | bytes 163872 | tf_op jit(solution)/shard_map/ppermute | solution.py:19
  15.7 1.3 fusion.45
  17.3 1.9 %copy-done.10 = bf16[1024,3072]{1,0:T(8,128)(2,1)S(1)} copy-done((bf16[1024,3072]{1,0:T(8,128)(2,1)S(1)}, bf16[1024,3072]{1,0:T(8,128)(2,1)}, u32[]{:S(2)}) %copy-start.10) | copy-done | bytes 6291480
  19.2 3.9 %convolution_convert_fusion.1 = bf16[512,3072]{1,0:T(8,128)(2,1)S(1)} fusion(bf16[1024,3072]{1,0:T(8,128)(2,1)S(1)} %copy-done.10, f32[512,1024]{1,0:T(8,128)S(1)} %get-tuple-element.153, f32[1024]{0:T(1024)S(1)} %get-tuple-element.118, f32[1024]{0:T(1024)S(1)} %get-tuple-element.119, f32[512]{0:T(512)S(1)} %add_rsqrt_fusion, f32[512]{0:T(512)S(1)} %broadcast_multiply_fusion), kind=kOutput, calls=%fused_computation.16 | convolution fusion | flops 3225419776 | bytes 11546624 | tf_op jit(solution)/shard_map/dot_general | solution.py:76
  23.3 1.3 pad_maximum_fusion.1
  24.6 0.5 copy-done.1
  25.1 6.6 %collective-permute-start.1 = (bf16[256,2048]{1,0:T(8,128)(2,1)}, bf16[256,2048]{1,0:T(8,128)(2,1)S(1)}, u32[]{:S(2)}, u32[]{:S(2)}) collective-permute-start(bf16[256,2048]{1,0:T(8,128)(2,1)} %pad_maximum_fusion.1), channel_id=1, source_target_pairs={{0,2},{1,3},{2,0},{3,1},{4,6},{5,7},{6,4},{7,5},{8,10},{9,11},{10,... | collective-permute-start | bytes 3145736 | tf_op jit(solution)/shard_map/ppermute | solution.py:19
  31.8 0.7 fusion.44
  32.6 0.7 fusion.43
  33.3 44.4 %collective-permute-done.1 = bf16[256,2048]{1,0:T(8,128)(2,1)S(1)} collective-permute-done((bf16[256,2048]{1,0:T(8,128)(2,1)}, bf16[256,2048]{1,0:T(8,128)(2,1)S(1)}, u32[]{:S(2)}, u32[]{:S(2)}) %collective-permute-start.1) | collective-permute-done | bytes 1048608 | tf_op jit(solution)/shard_map/ppermute | solution.py:19
  77.7 1.2 fusion.41
  78.9 1.9 %collective-permute-start.2 = (bf16[128,2048]{1,0:T(8,128)(2,1)}, bf16[128,2048]{1,0:T(8,128)(2,1)}, u32[]{:S(2)}, u32[]{:S(2)}) collective-permute-start(bf16[128,2048]{1,0:T(8,128)(2,1)} %get-tuple-element.115), channel_id=1, source_target_pairs={{0,4},{4,8},{8,12},{12,16},{16,20},{20,24},{24,28},{28,32},{32,36}... | collective-permute-start | bytes 1572872 | tf_op jit(solution)/shard_map/ppermute | solution.py:30
  80.8 6.7 %collective-permute-start.3 = (bf16[128,2048]{1,0:T(8,128)(2,1)}, bf16[128,2048]{1,0:T(8,128)(2,1)}, u32[]{:S(2)}, u32[]{:S(2)}) collective-permute-start(bf16[128,2048]{1,0:T(8,128)(2,1)} %get-tuple-element.116), channel_id=1, source_target_pairs={{4,0},{8,4},{12,8},{16,12},{20,16},{24,20},{28,24},{32,28},{36,32}... | collective-permute-start | bytes 1572872 | tf_op jit(solution)/shard_map/ppermute | solution.py:32
  87.5 10.2 %select_subtract_fusion = s32[512]{0:T(512)S(1)} fusion(s32[]{:T(128)} %bitcast.27, s32[]{:T(128)} %bitcast.26, s32[]{:T(128)} %bitcast.25, s32[]{:T(128)} %bitcast.24, s32[]{:T(128)} %bitcast.23, s32[]{:T(128)} %bitcast.22, s32[]{:T(128)} %bitcast.21, s32[]{:T(128)} %bitcast.20, s32[]{:T(128)} %bitcast.19, s32[]{:T(128)} %bitcast.18, s32[]{:T(128)} %bitcast.17, ...), kind=kLoop, calls=%fused_computation.61 | loop fusion | flops 28672 | bytes 4180 | tf_op jit(solution)/shard_map/sub | solution.py:86
  97.6 10.1 %select_add_fusion = s32[512]{0:T(512)S(1)} fusion(s32[]{:T(128)} %bitcast.43, s32[]{:T(128)} %bitcast.42, s32[]{:T(128)} %bitcast.41, s32[]{:T(128)} %bitcast.40, s32[]{:T(128)} %bitcast.39, s32[]{:T(128)} %bitcast.38, s32[]{:T(128)} %bitcast.37, s32[]{:T(128)} %bitcast.36, s32[]{:T(128)} %bitcast.35, s32[]{:T(128)} %bitcast.34, s32[]{:T(128)} %bitcast.33, ...), kind=kLoop, calls=%fused_computation.60 | loop fusion | flops 28672 | bytes 4180 | tf_op jit(solution)/shard_map/add | solution.py:87
  107.8 1.2 slice-done
  109.0 1.3 copy.17
  110.3 0.6 constant_dynamic-slice_fusion
  111.0 1.5 broadcast_select_fusion.1
  112.5 0.4 pad_maximum_fusion
  112.9 1.9 %fusion.39 = (bf16[768,1024]{1,0:T(8,128)(2,1)}, bf16[768,1024]{1,0:T(8,128)(2,1)}) fusion(bf16[768,2048]{1,0:T(8,128)(2,1)S(1)} %pad_maximum_fusion), kind=kLoop, calls=%fused_computation.94 | loop fusion | bytes 6291456 | tf_op jit(solution)/shard_map/slice | solution.py:165
  114.8 2.6 %copy.18 = bf16[768,1024]{0,1:T(8,128)(2,1)} copy(bf16[768,1024]{1,0:T(8,128)(2,1)} %get-tuple-element.110) | data formatting | bytes 3145728 | tf_op jit(solution)/shard_map/slice | solution.py:165
  117.5 2.7 %copy.19 = bf16[768,1024]{0,1:T(8,128)(2,1)} copy(bf16[768,1024]{1,0:T(8,128)(2,1)} %get-tuple-element.109) | data formatting | bytes 3145728 | tf_op jit(solution)/shard_map/slice | solution.py:165
  120.1 57.0 %while.13 = (s32[]{:T(128)}, bf16[16,512,64]{1,2,0:T(8,128)(2,1)S(1)}, bf16[16,512,64]{1,2,0:T(8,128)(2,1)}, bf16[16,768,64]{1,2,0:T(8,128)(2,1)}, bf16[16,768,6...) while((s32[]{:T(128)}, ...), condition=%wide.region_7.9_spmd.clone, body=%wide.region_4.8_spmd.clone.sunk | while | flops 105413632 | bytes 5066605 | solution.py:109
  120.1 1.6 fusion.61
  122.2 1.5 fusion.63
  123.7 1.6 fusion.61
  125.3 0.4 fusion.62
  125.7 1.5 fusion.63
  127.3 1.6 fusion.61
  129.3 1.5 fusion.63
  130.8 1.6 fusion.61
  132.9 1.5 fusion.63
  134.4 1.6 fusion.61
  136.4 1.5 fusion.63
  138.0 1.6 fusion.61
  140.0 1.5 fusion.63
  141.5 1.6 fusion.61
  143.6 1.5 fusion.63
  145.1 1.6 fusion.61
  147.1 1.5 fusion.63
  148.7 1.6 fusion.61
  150.7 1.5 fusion.63
  152.2 1.6 fusion.61
  154.3 1.5 fusion.63
  155.8 1.6 fusion.61
  157.8 1.5 fusion.63
  159.4 1.6 fusion.61
  161.4 1.5 fusion.63
  162.9 1.6 fusion.61
  165.0 1.5 fusion.63
  166.5 1.6 fusion.61
  168.5 1.5 fusion.63
  170.1 1.6 fusion.61
  172.1 1.5 fusion.63
  173.6 1.6 fusion.61
  175.7 1.5 fusion.63
  177.2 3.8 %add_convert_fusion = bf16[512,1024]{1,0:T(8,128)(2,1)} fusion(f32[512,1024]{1,0:T(8,128)} %copy-done.2, bf16[512,1024]{0,1:T(8,128)(2,1)S(1)} %bitcast.190, bf16[1024,1024]{1,0:T(8,128)(2,1)S(1)} %copy-done, f32[1024]{0:T(1024)S(1)} %get-tuple-element.117), kind=kOutput, calls=%fused_computation.24 | convolution fusion | flops 1075314688 | bytes 6295552 | tf_op jit(solution)/shard_map/dot_general | solution.py:166
  (64 shorter events, 6.8 us)
Async XLA Ops:
  0.6 176.6 %copy-start = (bf16[1024,1024]{1,0:T(8,128)(2,1)S(1)}, bf16[1024,1024]{1,0:T(8,128)(2,1)}, u32[]{:S(2)}) copy-start(bf16[1024,1024]{1,0:T(8,128)(2,1)} %param.31) | copy-start | bytes 6291460
  0.6 3.3 %copy-start.3 = (bf16[512,1024]{1,0:T(8,128)(2,1)S(1)}, bf16[512,1024]{1,0:T(8,128)(2,1)}, u32[]{:S(2)}) copy-start(bf16[512,1024]{1,0:T(8,128)(2,1)} %param.20) | copy-start | bytes 3145732
  0.7 3.3 %copy-start.11 = (bf16[1024,80]{0,1:T(8,128)(2,1)S(1)}, bf16[1024,80]{0,1:T(8,128)(2,1)}, u32[]{:S(2)}) copy-start(bf16[1024,80]{0,1:T(8,128)(2,1)} %param.26) | copy-start | bytes 491524
  3.9 7.1 %copy-start.6 = (bf16[80,1024]{1,0:T(8,128)(2,1)S(1)}, bf16[80,1024]{1,0:T(8,128)(2,1)}, u32[]{:S(2)}) copy-start(bf16[80,1024]{1,0:T(8,128)(2,1)} %param.28) | copy-start | bytes 491524
  3.9 7.1 %copy-start.8 = (f32[80,1024]{1,0:T(8,128)S(1)}, f32[80,1024]{1,0:T(8,128)}, u32[]{:S(2)}) copy-start(f32[80,1024]{1,0:T(8,128)} %param.22) | copy-start | bytes 983044
  4.5 11.1 %copy-start.7 = (f32[80,1024]{1,0:T(8,128)S(1)}, f32[80,1024]{1,0:T(8,128)}, u32[]{:S(2)}) copy-start(f32[80,1024]{1,0:T(8,128)} %param.21) | copy-start | bytes 983044
  4.5 11.1 %collective-permute-start = (f32[80,512]{1,0:T(8,128)S(1)}, f32[80,512]{1,0:T(8,128)S(1)}, u32[]{:S(2)}, u32[]{:S(2)}) collective-permute-start(f32[80,512]{1,0:T(8,128)S(1)} %convolution_bitcast_fusion), channel_id=1, source_target_pairs={{0,1},{1,0},{2,3},{3,2},{4,5},{5,4},{6,7},{7,6},{8,9},{9,8},{10,11... | collective-permute-start | bytes 491528 | tf_op jit(solution)/shard_map/ppermute | solution.py:19
  8.8 6.9 %copy-start.5 = (bf16[80,1024]{1,0:T(8,128)(2,1)S(1)}, bf16[80,1024]{1,0:T(8,128)(2,1)}, u32[]{:S(2)}) copy-start(bf16[80,1024]{1,0:T(8,128)(2,1)} %param.27) | copy-start | bytes 491524
  15.7 3.5 %copy-start.10 = (bf16[1024,3072]{1,0:T(8,128)(2,1)S(1)}, bf16[1024,3072]{1,0:T(8,128)(2,1)}, u32[]{:S(2)}) copy-start(bf16[1024,3072]{1,0:T(8,128)(2,1)} %param.30) | copy-start | bytes 18874372
  17.0 6.2 %copy-start.2 = (f32[512,1024]{1,0:T(8,128)}, f32[512,1024]{1,0:T(8,128)S(1)}, u32[]{:S(2)}) copy-start(f32[512,1024]{1,0:T(8,128)S(1)} %get-tuple-element.153) | copy-start | bytes 6291460
  23.2 1.9 %copy-start.1 = (bf16[512,3072]{1,0:T(8,128)(2,1)}, bf16[512,3072]{1,0:T(8,128)(2,1)S(1)}, u32[]{:S(2)}) copy-start(bf16[512,3072]{1,0:T(8,128)(2,1)S(1)} %convolution_convert_fusion.1) | copy-start | bytes 9437188
  23.2 8.5 %copy-start.12 = (s32[32]{0:T(128)S(1)}, s32[32]{0:T(128)}, u32[]{:S(2)}) copy-start(s32[32]{0:T(128)} %param.23) | copy-start | bytes 388
  23.2 8.6 %copy-start.13 = (s32[32]{0:T(128)S(1)}, s32[32]{0:T(128)}, u32[]{:S(2)}) copy-start(s32[32]{0:T(128)} %param.24) | copy-start | bytes 388
  23.3 64.2 %copy-start.9 = (s32[4,128]{1,0:T(4,128)S(1)}, s32[4,128]{1,0:T(4,128)}, u32[]{:S(2)}) copy-start(s32[4,128]{1,0:T(4,128)} %constant.213.clone.1) | copy-start | bytes 6148
  25.1 52.6 %collective-permute-start.1 = (bf16[256,2048]{1,0:T(8,128)(2,1)}, bf16[256,2048]{1,0:T(8,128)(2,1)S(1)}, u32[]{:S(2)}, u32[]{:S(2)}) collective-permute-start(bf16[256,2048]{1,0:T(8,128)(2,1)} %pad_maximum_fusion.1), channel_id=1, source_target_pairs={{0,2},{1,3},{2,0},{3,1},{4,6},{5,7},{6,4},{7,5},{8,10},{9,11},{10,... | collective-permute-start | bytes 3145736 | tf_op jit(solution)/shard_map/ppermute | solution.py:19
  77.7 30.1 %copy-start.4 = (bf16[256,2048]{1,0:T(8,128)(2,1)}, bf16[256,2048]{1,0:T(8,128)(2,1)S(1)}, u32[]{:S(2)}) copy-start(bf16[256,2048]{1,0:T(8,128)(2,1)S(1)} %collective-permute-done.1) | copy-start | bytes 3145732
  78.9 32.1 %collective-permute-start.2 = (bf16[128,2048]{1,0:T(8,128)(2,1)}, bf16[128,2048]{1,0:T(8,128)(2,1)}, u32[]{:S(2)}, u32[]{:S(2)}) collective-permute-start(bf16[128,2048]{1,0:T(8,128)(2,1)} %get-tuple-element.115), channel_id=1, source_target_pairs={{0,4},{4,8},{8,12},{12,16},{16,20},{20,24},{24,28},{28,32},{32,36}... | collective-permute-start | bytes 1572872 | tf_op jit(solution)/shard_map/ppermute | solution.py:30
  80.8 30.2 %collective-permute-start.3 = (bf16[128,2048]{1,0:T(8,128)(2,1)}, bf16[128,2048]{1,0:T(8,128)(2,1)}, u32[]{:S(2)}, u32[]{:S(2)}) collective-permute-start(bf16[128,2048]{1,0:T(8,128)(2,1)} %get-tuple-element.116), channel_id=1, source_target_pairs={{4,0},{8,4},{12,8},{16,12},{20,16},{24,20},{28,24},{32,28},{36,32}... | collective-permute-start | bytes 1572872 | tf_op jit(solution)/shard_map/ppermute | solution.py:32
  107.8 1.2 slice-start
  110.3 2.2 %slice-start.1 = ((bf16[512,3072]{1,0:T(8,128)(2,1)}), bf16[512,2048]{1,0:T(8,128)(2,1)S(1)}, s32[]{:S(2)}) async-start(bf16[512,3072]{1,0:T(8,128)(2,1)} %copy-done.1), calls=%async_computation.1 | async-start | bytes 4194304 | tf_op jit(solution)/shard_map/slice | solution.py:152
  117.5 2.7 %copy-start.14 = (bf16[16,512,64]{1,2,0:T(8,128)(2,1)S(1)}, bf16[16,512,64]{1,2,0:T(8,128)(2,1)}, u32[]{:S(2)}) copy-start(bf16[16,512,64]{1,2,0:T(8,128)(2,1)} %custom-call) | copy-start | bytes 3145732
where the time goes:
time: 183 us; the launch traced here: 181 us
  matrix products  63.3 us (35%)
  waiting for transfers between devices  48 us (26%)
  other arithmetic  33.6 us (18%)
  starting transfers between devices  18.5 us (10%)
  local copies, waits for them, and re-layouts  15.8 us (9%)
    ppermute x2, waiting for transfers between devices, from_partner(): lax.ppermute(shard, axis, [(i, i ^ 1 << distance) for i in range(lax.axis...  48 us
    dot_general x16, matrix products, one_head(): jnp.dot(query_one, key_one.T, preferred_element_type=jnp.float32)  26.2 us
    dot_general x16, matrix products, one_head(): jnp.dot(probs, value_one, preferred_element_type=jnp.float32)  24.2 us
    sub x1, other arithmetic, window_mask(): lower = (query_block - back_rows)[:, None]  10.2 us
    add x1, other arithmetic, window_mask(): upper = (query_block + ahead_rows)[:, None]  10.1 us
    ppermute x2, starting transfers between devices, from_partner(): lax.ppermute(shard, axis, [(i, i ^ 1 << distance) for i in range(lax.axis...  9.92 us
    ppermute x1, starting transfers between devices, padded(): lax.ppermute(head, axis, [((i + 1) % count, i) for i in range(ends)])  6.65 us
    reduce_sum x16, other arithmetic, one_head(): total = jnp.sum(weights, axis=-1, keepdims=True)  6.38 us
  transfers between devices with their start and end apart: 4, of which 2 were waited for; matrix products, arithmetic and copies ran while one was open for 15% of the time, Pallas kernels for 0%

commit v1 on v0

v1 whole, which is shorter than its diff:
```python
import functools
import math

import jax
import jax.numpy as jnp
from jax import lax
from jax.experimental import pallas as pl
from jax.experimental.pallas import tpu as pltpu
from jax.sharding import PartitionSpec as P

HEADS = 16
BLK = 32
NSTEPS = 32
HALO = 128
EPS = 1e-06
GUIDE = 0.5
TILE = 128
MASKED = -1e30
SMALL = 1e-30
LARGE = 1e30

F32 = jnp.float32
BF16 = jnp.bfloat16
VMEM_LIMIT = 48 * 1024 * 1024


def mm(a, b):
    return jnp.dot(a, b, preferred_element_type=F32)


def mm_nt(a, b):
    return lax.dot_general(a, b, (((1,), (1,)), ((), ())), preferred_element_type=F32)


def whole(memory_space=pltpu.VMEM):
    return pl.BlockSpec(memory_space=memory_space)


def time_value(step):
    return 1.0 - jnp.cos(0.5 * math.pi * step.astype(F32) / NSTEPS)


def time_features(step_index, freq):
    later = time_value(step_index[0] + 1)
    half_freq = freq // 2
    freqs = jnp.exp(-math.log(10000.0) * jnp.arange(half_freq, dtype=F32) / half_freq)
    angles = 1000.0 * later * freqs
    return jnp.concatenate([jnp.sin(angles), jnp.cos(angles)])[None, :]


def velocity_kernel(hidden_ref, weight_ref, vel_ref, sent_ref):
    rows = hidden_ref[...].astype(F32)
    mean = jnp.mean(rows, axis=-1, keepdims=True)
    centered = rows - mean
    spread = jnp.mean(centered * centered, axis=-1, keepdims=True)
    normed = (centered * lax.rsqrt(spread + EPS)).astype(BF16)
    vel = mm(normed, weight_ref[...]).T
    vel_ref[...] = vel
    sent_ref[...] = vel.astype(BF16)


def velocity_call(hidden, proj_weight):
    rows, width = hidden.shape
    mel = proj_weight.shape[1]
    step = 128
    return pl.pallas_call(
        velocity_kernel,
        grid=(rows // step,),
        in_specs=[
            pl.BlockSpec((step, width), lambda i: (i, 0)),
            pl.BlockSpec((width, mel), lambda i: (0, 0)),
        ],
        out_specs=[
            pl.BlockSpec((mel, step), lambda i: (0, i)),
            pl.BlockSpec((mel, step), lambda i: (0, i)),
        ],
        out_shape=[
            jax.ShapeDtypeStruct((mel, rows), F32),
            jax.ShapeDtypeStruct((mel, rows), BF16),
        ],
        cost_estimate=pl.CostEstimate(
            flops=2 * rows * width * mel, bytes_accessed=2 * rows * width, transcendentals=0
        ),
        name="velocity",
    )(hidden, proj_weight)


def prepare_kernel(
    ints_ref,
    back_ref,
    ahead_ref,
    feats_ref,
    latent_w_ref,
    prompt_w_ref,
    time_w_ref,
    qkv_ref,
    mixed_ref,
    keyed_ref,
    gram_ref,
    embed_ref,
    gate_ref,
    bias_ref,
    left_ref,
):
    step = pl.program_id(0)
    mel, width = latent_w_ref.shape

    @pl.when(step == 0)
    def _():
        feats = feats_ref[...]
        high = feats.astype(BF16)
        rest = feats - high.astype(F32)
        mid = rest.astype(BF16)
        low = (rest - mid.astype(F32)).astype(BF16)
        stacked = jnp.concatenate([high, mid, low], axis=0)
        parts = mm(stacked, time_w_ref[...])
        freq_rows = high.shape[0]
        mod = parts[0:1] + (
            parts[freq_rows : freq_rows + 1] + parts[2 * freq_rows : 2 * freq_rows + 1]
        )
        shift, scale, gate = mod[:, :width], mod[:, width : 2 * width], mod[:, 2 * width :]
        gate_ref[...] = gate
        both = jnp.concatenate([latent_w_ref[...], prompt_w_ref[...]], axis=0)
        embed = jnp.concatenate(
            [both, latent_w_ref[...], jnp.zeros((256 - 3 * mel, width), BF16)], axis=0
        )
        embed_ref[...] = embed
        wide = both.astype(F32)
        centered = wide - jnp.mean(wide, axis=-1, keepdims=True)
        left_ref[0 : 2 * mel] = (centered * (1.0 + scale)).astype(BF16)
        shift_high = shift.astype(BF16).astype(F32)
        which = lax.broadcasted_iota(jnp.int32, (16, width), 0)
        left_ref[2 * mel : 2 * mel + 16] = jnp.where(
            which == 0, shift_high, jnp.where(which == 1, shift - shift_high, 0.0)
        ).astype(BF16)
        col = jnp.mean(embed.astype(F32), axis=-1, keepdims=True)
        row = mm_nt(jnp.ones((16, width), BF16), embed)[0:1] / width
        gram = mm_nt(embed, embed) / width - col * row
        gram_high = gram.astype(BF16)
        gram_ref[0:256] = gram_high
        gram_ref[256:512] = (gram - gram_high.astype(F32)).astype(BF16)
        half = ints_ref[0]
        first_block = ints_ref[2]
        total_blocks = ints_ref[3]
        per_half = back_ref.shape[0] // 2
        keys = bias_ref.shape[1]
        row_block = lax.broadcasted_iota(jnp.int32, (16, keys), 0)
        lower = jnp.zeros((16, keys), jnp.int32)
        upper = jnp.zeros((16, keys), jnp.int32)
        for block in range(per_half):
            lower = jnp.where(row_block == block, block - back_ref[half * per_half + block], lower)
            upper = jnp.where(row_block == block, block + ahead_ref[half * per_half + block], upper)
        key_block = lax.broadcasted_iota(jnp.int32, (16, keys), 1) // BLK - HALO // BLK
        place = key_block + first_block
        seen = (key_block >= lower) & (key_block <= upper) & (place >= 0) & (place < total_blocks)
        bias_ref[0:16] = jnp.where(seen, 0.0, MASKED).astype(BF16)
        bias_ref[16:128] = jnp.zeros((112, keys), BF16)

    acc = mm(left_ref[...], qkv_ref[...])
    columns = acc.shape[1]
    acc = acc * jnp.where(step < 2, math.log2(math.e) / math.sqrt(width // HEADS), 1.0)
    offset = acc[2 * mel : 2 * mel + 1] + acc[2 * mel + 1 : 2 * mel + 2]
    offset_high = offset.astype(BF16).astype(F32)
    which = lax.broadcasted_iota(jnp.int32, (256 - 3 * mel, columns), 0)
    last = jnp.where(which == 0, offset_high, jnp.where(which == 1, offset - offset_high, 0.0))
    block = jnp.concatenate([acc[: 2 * mel], acc[:mel], last], axis=0)
    mixed_ref[...] = block.astype(BF16)

    @pl.when((step == 2) | (step == 3))
    def _():
        keyed_ref[...] = block.T.astype(BF16)


def prepare_call(ints, back, ahead, feats, latent_weight, prompt_weight, time_weight, qkv_weight):
    mel, width = latent_weight.shape
    step = 512
    steps = 3 * width // step
    fixed = lambda j: (0, 0)
    smem = pl.BlockSpec(memory_space=pltpu.SMEM)
    return pl.pallas_call(
        prepare_kernel,
        grid=(steps,),
        in_specs=[
            smem,
            smem,
            smem,
            pl.BlockSpec(feats.shape, fixed),
            pl.BlockSpec((mel, width), fixed),
            pl.BlockSpec((mel, width), fixed),
            pl.BlockSpec(time_weight.shape, fixed),
            pl.BlockSpec((width, step), lambda j: (0, j)),
        ],
        out_specs=[
            pl.BlockSpec((256, step), lambda j: (0, j)),
            pl.BlockSpec((step, 256), lambda j: (jnp.clip(j - 2, 0, 1), 0)),
            pl.BlockSpec((512, 256), fixed),
            pl.BlockSpec((256, width), fixed),
            pl.BlockSpec((1, width), fixed),
            pl.BlockSpec((128, 512 + 2 * HALO), fixed),
        ],
        out_shape=[
            jax.ShapeDtypeStruct((256, 3 * width), BF16),
            jax.ShapeDtypeStruct((width, 256), BF16),
            jax.ShapeDtypeStruct((512, 256), BF16),
            jax.ShapeDtypeStruct((256, width), BF16),
            jax.ShapeDtypeStruct((1, width), F32),
            jax.ShapeDtypeStruct((128, 512 + 2 * HALO), BF16),
        ],
        scratch_shapes=[pltpu.VMEM((2 * mel + 16, width), BF16)],
        compiler_params=pltpu.CompilerParams(vmem_limit_bytes=VMEM_LIMIT),
        cost_estimate=pl.CostEstimate(
            flops=2 * 256 * width * 3 * width, bytes_accessed=8 * width * width, transcendentals=0
        ),
        name="prepare",
    )(ints, back, ahead, feats, latent_weight, prompt_weight, time_weight, qkv_weight)


def combine_kernel(
    ints_ref,
    floats_ref,
    vel_ref,
    partner_ref,
    latent_ref,
    prompt_ref,
    next_ref,
    rows_ref,
    seq_ref,
    cross_ref,
):
    half, branch = ints_ref[0], ints_ref[1]
    mel, frames = vel_ref.shape
    updated = latent_ref[...] + (
        floats_ref[0] * vel_ref[...] + floats_ref[1] * partner_ref[...].astype(F32)
    )
    share = frames // 2
    next_ref[...] = jnp.where(branch == 0, updated[:, :share], updated[:, share:])
    high = updated.astype(BF16)
    rows_ref[0:mel] = high
    prompt = prompt_ref[...]
    rows_ref[mel : 2 * mel] = (prompt * floats_ref[2]).astype(BF16)
    rows_ref[2 * mel : 3 * mel] = (updated - high.astype(F32)).astype(BF16)
    rows_ref[3 * mel : 256] = jnp.zeros((256 - 3 * mel, frames), BF16)
    head, tail = updated[:, :HALO], updated[:, frames - HALO :]
    seq_ref[0:mel] = jnp.where(half == 0, head, tail).astype(BF16)
    seq_ref[mel : 2 * mel] = jnp.where(
        half == 0, prompt[:, :HALO], prompt[:, frames - HALO :]
    ).astype(BF16)
    cross_ref[...] = jnp.where(half == 0, tail, head).astype(BF16)


def combine_call(ints, floats, vel, partner, latent, prompt):
    mel, frames = vel.shape
    fixed = lambda i, ints: (0, 0)
    mine = lambda i, ints: (0, ints[0])
    return pl.pallas_call(
        combine_kernel,
        grid_spec=pltpu.PrefetchScalarGridSpec(
            num_scalar_prefetch=1,
            grid=(1,),
            in_specs=[
                pl.BlockSpec(memory_space=pltpu.SMEM),
                pl.BlockSpec((mel, frames), fixed),
                pl.BlockSpec((mel, frames), fixed),
                pl.BlockSpec((mel, frames), mine),
                pl.BlockSpec((mel, frames), mine),
            ],
            out_specs=[
                pl.BlockSpec((mel, frames // 2), fixed),
                pl.BlockSpec((256, frames), fixed),
                pl.BlockSpec((2 * mel, HALO), fixed),
                pl.BlockSpec((mel, HALO), fixed),
            ],
        ),
        out_shape=[
            jax.ShapeDtypeStruct((mel, frames // 2), F32),
            jax.ShapeDtypeStruct((256, frames), BF16),
            jax.ShapeDtypeStruct((2 * mel, HALO), BF16),
            jax.ShapeDtypeStruct((mel, HALO), BF16),
        ],
        name="combine",
    )(ints, floats, vel, partner, latent, prompt)


def layer_kernel(
    ints_ref,
    floats_ref,
    own_ref,
    seq_ref,
    cross_ref,
    prompt_ref,
    mixed_ref,
    keyed_ref,
    gram_ref,
    embed_ref,
    bias_ref,
    gate_ref,
    out_w_ref,
    next_ref,
    query_ref,
    key_ref,
    value_ref,
    context_ref,
):
    half = ints_ref[0]
    flag = floats_ref[2]
    mel = cross_ref.shape[0]
    frames = own_ref.shape[1]
    width = embed_ref.shape[1]
    keys = frames + 2 * HALO
    pairs = width // 128
    own = own_ref[...]
    blank = jnp.zeros((256 - 2 * mel, HALO), F32)
    seq_rows = jnp.concatenate(
        [seq_ref[0:mel].astype(F32), seq_ref[mel : 2 * mel].astype(F32) * flag, blank], axis=0
    )
    cross_rows = jnp.concatenate(
        [cross_ref[...].astype(F32), prompt_ref[...] * flag, blank], axis=0
    )
    before = jnp.where(half == 0, seq_rows, cross_rows).astype(BF16)
    after = jnp.where(half == 0, cross_rows, seq_rows).astype(BF16)
    rows = jnp.concatenate([before, own, after], axis=1)
    weighted = mm(gram_ref[0:256], rows) + mm(gram_ref[256:512], rows)
    rows = rows.astype(F32)
    spread = jnp.sum(weighted * rows, axis=0, keepdims=True)
    inverse = lax.rsqrt(jnp.maximum(spread, 0.0) + EPS)
    latent = (rows[0:mel] + rows[2 * mel : 3 * mel]) * inverse
    high = latent.astype(BF16)
    which = lax.broadcasted_iota(jnp.int32, (256 - 3 * mel, keys), 0)
    normed = jnp.concatenate(
        [
            high,
            (rows[mel : 2 * mel] * inverse).astype(BF16),
            (latent - high.astype(F32)).astype(BF16),
            jnp.where(which < 2, 1.0, 0.0).astype(BF16),
        ],
        axis=0,
    )
    turned = normed.T
    for start in range(0, width, 256):
        cols = slice(start, start + 256)
        key_ref[cols] = mm(keyed_ref[cols], normed).astype(BF16)
        value_ref[:, cols] = mm(turned, mixed_ref[:, 2 * width + start : 2 * width + start + 256]).astype(BF16)
        query_ref[:, cols] = mm(turned[HALO : HALO + frames], mixed_ref[:, cols]).astype(BF16)

    lane = lax.broadcasted_iota(jnp.int32, (TILE, 128), 1)
    row = lax.broadcasted_iota(jnp.int32, (TILE, 128), 0)
    left = lane < 64
    ones = jnp.ones((TILE + 2 * HALO, 128), BF16)

    def attend(tile, pair, stable):
        at = tile * TILE
        cols = pl.ds(pair * 128, 128)
        window = pl.ds(at, TILE + 2 * HALO)
        query = query_ref[pl.ds(at, TILE), cols]
        zero = jnp.zeros_like(query)
        chosen = (lane == tile * (TILE // BLK) + row // BLK).astype(F32).astype(BF16)
        stacked = jnp.concatenate(
            [
                jnp.concatenate([jnp.where(left, query, zero), chosen], axis=1),
                jnp.concatenate([jnp.where(left, zero, query), chosen], axis=1),
            ],
            axis=0,
        )
        right = jnp.concatenate([key_ref[cols, window], bias_ref[:, window]], axis=0)
        scores = mm(stacked, right)
        if stable:
            scores = scores - jnp.max(scores, axis=-1, keepdims=True)
        probs = jnp.exp2(scores).astype(BF16)
        values = jnp.concatenate([value_ref[window, cols], ones], axis=1)
        both = mm(probs, values)
        total = jnp.where(left, both[:TILE, 128:], both[TILE:, 128:])
        context = jnp.where(left, both[:TILE, :128], both[TILE:, :128]) / total
        context_ref[pl.ds(at, TILE), cols] = context.astype(BF16)
        return total

    least = jnp.full((TILE, 128), 1.0, F32)
    most = jnp.full((TILE, 128), 1.0, F32)
    for tile in range(frames // TILE):
        for pair in range(pairs):
            total = attend(tile, pair, False)
            least = jnp.minimum(least, total)
            most = jnp.maximum(most, total)
    safe = (jnp.min(least) > SMALL) & (jnp.max(most) < LARGE)

    @pl.when(jnp.logical_not(safe))
    def _():
        def one(index, carry):
            attend(index // pairs, index % pairs, True)
            return carry

        lax.fori_loop(0, frames // TILE * pairs, one, 0)

    own_turned = own.T
    gate = gate_ref[...]
    for start in range(0, width, 256):
        cols = slice(start, start + 256)
        first = mm(own_turned, embed_ref[:, cols])
        projected = mm(context_ref[...], out_w_ref[:, cols])
        next_ref[:, cols] = (first + gate[:, cols] * projected).astype(BF16)


def layer_call(ints, floats, own, seq, cross, prompt, mixed, keyed, gram, embed, bias, gate, out_w):
    mel = cross.shape[0]
    frames = own.shape[1]
    width = embed.shape[1]
    keys = frames + 2 * HALO
    fixed = lambda i, ints: (0, 0)
    blocks = frames // HALO

    def full(array):
        return pl.BlockSpec(array.shape, fixed)

    return pl.pallas_call(
        layer_kernel,
        grid_spec=pltpu.PrefetchScalarGridSpec(
            num_scalar_prefetch=1,
            grid=(1,),
            in_specs=[
                pl.BlockSpec(memory_space=pltpu.SMEM),
                full(own),
                full(seq),
                full(cross),
                pl.BlockSpec((mel, HALO), lambda i, ints: (0, blocks - ints[0])),
                full(mixed),
                full(keyed),
                full(gram),
                full(embed),
                full(bias),
                full(gate),
                full(out_w),
            ],
            out_specs=pl.BlockSpec((frames, width), fixed),
            scratch_shapes=[
                pltpu.VMEM((frames, width), BF16),
                pltpu.VMEM((width, keys), BF16),
                pltpu.VMEM((keys, width), BF16),
                pltpu.VMEM((frames, width), BF16),
            ],
        ),
        out_shape=jax.ShapeDtypeStruct((frames, width), BF16),
        compiler_params=pltpu.CompilerParams(vmem_limit_bytes=VMEM_LIMIT),
        cost_estimate=pl.CostEstimate(
            flops=4_000_000_000, bytes_accessed=6_000_000, transcendentals=3_000_000
        ),
        name="layer",
    )(ints, floats, own, seq, cross, prompt, mixed, keyed, gram, embed, bias, gate, out_w)


def body(
    hidden,
    latent,
    prompt_mel,
    window_back,
    window_ahead,
    step_index,
    proj_weight,
    latent_weight,
    prompt_weight,
    time_weight,
    qkv_weight,
    attn_out_weight,
):
    axes = ("seq", "cfg")
    spans = lax.axis_size("seq")
    rows, width = hidden.shape
    place = lax.axis_index("cfg")
    branch, half = place % 2, place // 2
    first_block = (2 * lax.axis_index("seq") + half) * (rows // BLK)
    total_blocks = 2 * spans * (rows // BLK)
    ints = jnp.stack([half, branch, first_block, jnp.int32(total_blocks)]).astype(jnp.int32)
    delta = time_value(step_index[0] + 1) - time_value(step_index[0])
    mine = jnp.where(branch == 0, 1.0 + GUIDE, -GUIDE)
    other = jnp.where(branch == 0, -GUIDE, 1.0 + GUIDE)
    flag = jnp.where(branch == 0, 1.0, 0.0)
    floats = jnp.stack([delta * mine, delta * other, flag]).astype(F32)

    def at(span, cell):
        return span * 4 + cell

    everyone = [(span, cell) for span in range(spans) for cell in range(4)]
    to_partner = [(at(s, c), at(s, c ^ 1)) for s, c in everyone]
    to_half = [(at(s, c), at(s, c ^ 3)) for s, c in everyone]
    to_seq = [
        (at(s, c), at(s + (1 if c >= 2 else -1), c ^ 3))
        for s, c in everyone
        if 0 <= s + (1 if c >= 2 else -1) < spans
    ]
    vel, sent = velocity_call(hidden, proj_weight)
    partner = lax.ppermute(sent, axes, to_partner)
    feats = jnp.broadcast_to(time_features(step_index, time_weight.shape[0]), (16, time_weight.shape[0]))
    mixed, keyed, gram, embed, gate, bias = prepare_call(
        ints, window_back, window_ahead, feats, latent_weight, prompt_weight, time_weight, qkv_weight
    )
    latent_out, own, seq, cross = combine_call(ints, floats, vel, partner, latent, prompt_mel)
    cross = lax.ppermute(cross, axes, to_half)
    seq = lax.ppermute(seq, axes, to_seq)
    hidden_next = layer_call(
        ints, floats, own, seq, cross, prompt_mel, mixed, keyed, gram, embed, bias, gate, attn_out_weight
    )
    return (latent_out, hidden_next)


def solution(mesh):
    in_specs = (
        P(("seq", "cfg"), None),
        P(None, "seq"),
        P(None, "seq"),
        P("seq"),
        P("seq"),
        P(),
        P(),
        P(),
        P(),
        P(),
        P(),
        P(),
    )
    out_specs = (P(None, ("seq", "cfg")), P(("seq", "cfg"), None))
    return jax.shard_map(body, mesh=mesh, in_specs=in_specs, out_specs=out_specs, check_vma=False)
```

time: 183 us -> 59.5 us (0.33)
  matrix products: 63.3 us -> 0 us
  waiting for transfers between devices: 48 us -> 2.27 us
  Pallas kernels: 0 us -> 38.6 us
  other arithmetic: 33.6 us -> 1.29 us
  local copies, waits for them, and re-layouts: 15.8 us -> 3.13 us
  starting transfers between devices: 18.5 us -> 12.3 us
    dot_general x38 -> x0, matrix products: 63.3 us -> none  [the longest x16 26.2 us: one_head(): jnp.dot(query_one, key_one.T, preferred_element_type=jnp.float32)]
    ppermute x4 -> x3, waiting for transfers between devices: 48 us -> 2.27 us  [the longest x1 2.27 us: body(): partner = lax.ppermute(sent, axes, to_partner)]
    pallas_call x0 -> x4, Pallas kernels: none -> 38.6 us  [the longest x1 25.1 us: layer_call(): pl.pallas_call(layer_kernel, grid_spec=pltpu.PrefetchScalarGridSpec(num_s...]
    slice x10 -> x0, local copies, waits for them, and re-layouts: 11.1 us -> none  [the longest x2 4.61 us: body(): window[:, width:]]
    sub x1 -> x0, other arithmetic: 10.2 us -> none  [window_mask(): lower = (query_block - back_rows)[:, None]]
    add x2 -> x0, other arithmetic: 10.1 us -> none  [the longest x1 10.1 us: window_mask(): upper = (query_block + ahead_rows)[:, None]]
    reduce_sum x19 -> x0, other arithmetic: 9.95 us -> none  [the longest x16 6.38 us: one_head(): total = jnp.sum(weights, axis=-1, keepdims=True)]
    ppermute x4 -> x3, starting transfers between devices: 18.5 us -> 12.3 us  [the longest x1 4.84 us: body(): seq = lax.ppermute(seq, axes, to_seq)]
  transfers between devices with their start and end apart: 4 -> 3, of which waited for: 2 -> 1; matrix products, arithmetic and copies ran while one was open for 15% -> 2% of each run, Pallas kernels for 0% -> 11%
where the time goes in v1:
time: 59.5 us; the launch traced here: 59.2 us
  Pallas kernels  38.6 us (65%)
  starting transfers between devices  12.3 us (21%)
  local copies, waits for them, and re-layouts  3.13 us (5%)
  waiting for transfers between devices  2.27 us (4%)
  between operations  1.65 us (3%)
  other arithmetic  1.29 us (2%)
    pallas_call x1, Pallas kernels, layer_call(): pl.pallas_call(layer_kernel, grid_spec=pltpu.PrefetchScalarGridSpec(num_s...  25.1 us
    pallas_call x1, Pallas kernels, prepare_call(): pl.pallas_call(prepare_kernel, grid=(steps,), in_specs=[smem, smem, smem,...  6.7 us
    ppermute x1, starting transfers between devices, body(): seq = lax.ppermute(seq, axes, to_seq)  4.84 us
    pallas_call x1, Pallas kernels, velocity_call(): pl.pallas_call(velocity_kernel, grid=(rows // step,), in_specs=[pl.BlockS...  4.2 us
    ppermute x1, starting transfers between devices, body(): cross = lax.ppermute(cross, axes, to_half)  4.17 us
    ppermute x1, starting transfers between devices, body(): partner = lax.ppermute(sent, axes, to_partner)  3.27 us
    unnamed x23, local copies, waits for them, and re-layouts  3.13 us
    pallas_call x1, Pallas kernels, combine_call(): pl.pallas_call(combine_kernel, grid_spec=pltpu.PrefetchScalarGridSpec(num...  2.57 us
  transfers between devices with their start and end apart: 3, of which 1 were waited for; matrix products, arithmetic and copies ran while one was open for 2% of the time, Pallas kernels for 11%

profile of v1, /device:TPU:6, one launch (start us, length us, event | category | flops | bytes accessed | tf_op | source)
XLA Modules:
  0.0 59.2 jit_solution(1285303913800395273)
XLA Ops:
  0.6 0.0 copy-start
  0.6 0.0 copy-start.3
  0.7 0.0 copy-start.2
  0.7 0.0 copy-start.7
  0.7 0.0 copy-start.6
  0.7 1.9 %copy.14.weight_ref = bf16[1024,80]{1,0:T(8,128)(2,1)} copy(bf16[1024,80]{0,1:T(8,128)(2,1)} %param.18) | data formatting | bytes 327680 | tf_op args[6]
  2.6 4.2 %velocity.1 = (f32[80,512]{1,0:T(8,128)}, bf16[80,512]{1,0:T(8,128)(2,1)}) custom-call(bf16[512,1024]{1,0:T(8,128)(2,1)} %hidden_ref.1, bf16[1024,80]{1,0:T(8,128)(2,1)} %copy.14.weight_ref), custom_call_target="tpu_custom_call" | custom-call | flops 83886080 | bytes 1048576 | tf_op jit(solution)/shard_map/velocity/pallas_call | solution.py:66
  6.8 3.3 %collective-permute-start = (bf16[80,512]{1,0:T(8,128)(2,1)}, bf16[80,512]{1,0:T(8,128)(2,1)S(1)}, u32[]{:S(2)}, u32[]{:S(2)}) collective-permute-start(bf16[80,512]{1,0:T(8,128)(2,1)} %get-tuple-element.15), channel_id=1, source_target_pairs={{0,1},{1,0},{2,3},{3,2},{4,5},{5,4},{6,7},{7,6},{8,9},{9,8},{10,11... | collective-permute-start | bytes 245768 | tf_op jit(solution)/shard_map/ppermute | solution.py:489
  10.9 0.7 %pad_maximum_fusion.1.floats_ref = f32[3]{0:T(128)} fusion(f32[1]{0:T(128)} %bitcast.6, f32[1]{0:T(128)} %bitcast.5, f32[1]{0:T(128)} %bitcast.4), kind=kLoop, calls=%fused_computation.2 | loop fusion | flops 6 | bytes 24 | tf_op jit(solution)/shard_map/stack | solution.py:475
  11.6 0.6 pad_add_fusion.ints_ref
  12.2 2.3 %collective-permute-done.partner_ref = bf16[80,512]{1,0:T(8,128)(2,1)S(1)} collective-permute-done((bf16[80,512]{1,0:T(8,128)(2,1)}, bf16[80,512]{1,0:T(8,128)(2,1)S(1)}, u32[]{:S(2)}, u32[]{:S(2)}) %collective-permute-start) | collective-permute-done | bytes 81952 | tf_op jit(solution)/shard_map/ppermute | solution.py:489
  14.5 0.0 copy-start.10
  14.5 0.6 %copy-done.10 = bf16[80,512]{1,0:T(8,128)(2,1)} copy-done((bf16[80,512]{1,0:T(8,128)(2,1)}, bf16[80,512]{1,0:T(8,128)(2,1)S(1)}, u32[]{:S(2)}) %copy-start.10) | copy-done | bytes 81944
  15.1 2.6 %combine.1 = (f32[80,256]{1,0:T(8,128)}, bf16[256,512]{1,0:T(8,128)(2,1)}, bf16[160,128]{1,0:T(8,128)(2,1)}, bf16[80,128]{1,0:T(8,128)(2,1)}) custom-call(s32[4]{0:T(128)} %pad_add_fusion.ints_ref, f32[3]{0:T(128)} %pad_maximum_fusion.1.floats_ref, f32[80,512]{1,0:T(8,128)} %get-tuple-element.14.vel_ref, bf16[80,512]{1,0:T(8,128)(2,1)} %copy-done.10, ...), custom_call_target="tpu_custom_call" | custom-call | tf_op jit(solution)/shard_map/combine/pallas_call | solution.py:255
  17.6 4.2 %collective-permute-start.2 = (bf16[80,128]{1,0:T(8,128)(2,1)}, bf16[80,128]{1,0:T(8,128)(2,1)S(1)}, u32[]{:S(2)}, u32[]{:S(2)}) collective-permute-start(bf16[80,128]{1,0:T(8,128)(2,1)} %get-tuple-element.19), channel_id=1, source_target_pairs={{0,3},{1,2},{2,1},{3,0},{4,7},{5,6},{6,5},{7,4},{8,11},{9,10},{10,... | collective-permute-start | bytes 61448 | tf_op jit(solution)/shard_map/ppermute | solution.py:495
  21.8 4.8 %collective-permute-start.1 = (bf16[160,128]{1,0:T(8,128)(2,1)}, bf16[160,128]{1,0:T(8,128)(2,1)S(1)}, u32[]{:S(2)}, u32[]{:S(2)}) collective-permute-start(bf16[160,128]{1,0:T(8,128)(2,1)} %get-tuple-element.18), channel_id=1, source_target_pairs={{2,5},{3,4},{4,3},{5,2},{6,9},{7,8},{8,7},{9,6},{10,13},{11,12},{1... | collective-permute-start | bytes 122888 | tf_op jit(solution)/shard_map/ppermute | solution.py:496
  26.7 0.0 copy-done
  26.7 0.0 copy-done.3
  26.7 0.0 copy-done.2
  26.7 0.0 copy-done.7
  26.7 0.0 copy-done.6
  26.7 0.0 copy-start.4
  26.7 0.6 copy-done.4
  27.3 0.0 copy-start.1
  27.3 0.0 copy-start.5
  27.3 0.0 copy-start.8
  27.3 0.0 copy-start.9
  27.3 6.7 %prepare.1 = (bf16[256,3072]{1,0:T(8,128)(2,1)S(1)}, bf16[1024,256]{1,0:T(8,128)(2,1)S(1)}, bf16[512,256]{1,0:T(8,128)(2,1)S(1)}, bf16[256,1024]{1,0:T(8,128)(2,...) custom-call(s32[4]{0:T(128)S(1)} %copy-done.4, s32[32]{0:T(128)S(1)} %copy-done.6, s32[32]{0:T(128)S(1)} %copy-done.7, ...), custom_call_target="tpu_custom_call" | custom-call | flops 1610612736 | bytes 8388608 | tf_op jit(solution)/shard_map/prepare/pallas_call | solution.py:180
  34.0 0.0 collective-permute-done.2.cross_ref
  34.1 0.0 collective-permute-done.1.seq_ref
  34.1 0.0 copy-done.1
  34.1 0.0 copy-done.5
  34.1 0.0 copy-done.8
  34.1 0.0 copy-done.9
  34.1 25.1 %layer.1 = bf16[512,1024]{1,0:T(8,128)(2,1)} custom-call(s32[4]{0:T(128)S(1)} %copy-done.4, f32[3]{0:T(128)S(1)} %copy-done.5, bf16[256,512]{1,0:T(8,128)(2,1)S(1)} %copy-done.9, bf16[160,128]{1,0:T(8,128)(2,1)S(1)} %collective-permute-done.1.seq_ref, bf16[80,128]{1,0:T(8,128)(2,1)S(1)} %collective-permute-done.2.cross_ref, f32[80,1024]{1,0:T(8,128)S(1)} %copy-done.1, ...), custom_call_target="tpu_custom_call" | custom-call | flops 4000000000 | bytes 6000000 | tf_op jit(solution)/shard_map/layer/pallas_call | solution.py:413
  (3 shorter events, 0.1 us)
Async XLA Ops:
  0.6 26.0 %copy-start = (bf16[256,3072]{1,0:T(8,128)(2,1)S(1)}, bf16[256,3072]{1,0:T(8,128)(2,1)}, u32[]{:S(2)}) copy-start(bf16[256,3072]{1,0:T(8,128)(2,1)} %time_w_ref.1) | copy-start | bytes 4718596
  0.6 26.0 %copy-start.3 = (bf16[80,1024]{1,0:T(8,128)(2,1)S(1)}, bf16[80,1024]{1,0:T(8,128)(2,1)}, u32[]{:S(2)}) copy-start(bf16[80,1024]{1,0:T(8,128)(2,1)} %prompt_w_ref.1) | copy-start | bytes 491524
  0.7 26.0 %copy-start.2 = (bf16[80,1024]{1,0:T(8,128)(2,1)S(1)}, bf16[80,1024]{1,0:T(8,128)(2,1)}, u32[]{:S(2)}) copy-start(bf16[80,1024]{1,0:T(8,128)(2,1)} %latent_w_ref.1) | copy-start | bytes 491524
  0.7 26.0 %copy-start.7 = (s32[32]{0:T(128)S(1)}, s32[32]{0:T(128)}, u32[]{:S(2)}) copy-start(s32[32]{0:T(128)} %ahead_ref.1) | copy-start | bytes 388
  0.7 26.0 %copy-start.6 = (s32[32]{0:T(128)S(1)}, s32[32]{0:T(128)}, u32[]{:S(2)}) copy-start(s32[32]{0:T(128)} %back_ref.1) | copy-start | bytes 388
  6.8 7.7 %collective-permute-start = (bf16[80,512]{1,0:T(8,128)(2,1)}, bf16[80,512]{1,0:T(8,128)(2,1)S(1)}, u32[]{:S(2)}, u32[]{:S(2)}) collective-permute-start(bf16[80,512]{1,0:T(8,128)(2,1)} %get-tuple-element.15), channel_id=1, source_target_pairs={{0,1},{1,0},{2,3},{3,2},{4,5},{5,4},{6,7},{7,6},{8,9},{9,8},{10,11... | collective-permute-start | bytes 245768 | tf_op jit(solution)/shard_map/ppermute | solution.py:489
  14.5 0.6 %copy-start.10 = (bf16[80,512]{1,0:T(8,128)(2,1)}, bf16[80,512]{1,0:T(8,128)(2,1)S(1)}, u32[]{:S(2)}) copy-start(bf16[80,512]{1,0:T(8,128)(2,1)S(1)} %collective-permute-done.partner_ref) | copy-start | bytes 245764
  17.6 16.4 %collective-permute-start.2 = (bf16[80,128]{1,0:T(8,128)(2,1)}, bf16[80,128]{1,0:T(8,128)(2,1)S(1)}, u32[]{:S(2)}, u32[]{:S(2)}) collective-permute-start(bf16[80,128]{1,0:T(8,128)(2,1)} %get-tuple-element.19), channel_id=1, source_target_pairs={{0,3},{1,2},{2,1},{3,0},{4,7},{5,6},{6,5},{7,4},{8,11},{9,10},{10,... | collective-permute-start | bytes 61448 | tf_op jit(solution)/shard_map/ppermute | solution.py:495
  21.8 12.2 %collective-permute-start.1 = (bf16[160,128]{1,0:T(8,128)(2,1)}, bf16[160,128]{1,0:T(8,128)(2,1)S(1)}, u32[]{:S(2)}, u32[]{:S(2)}) collective-permute-start(bf16[160,128]{1,0:T(8,128)(2,1)} %get-tuple-element.18), channel_id=1, source_target_pairs={{2,5},{3,4},{4,3},{5,2},{6,9},{7,8},{8,7},{9,6},{10,13},{11,12},{1... | collective-permute-start | bytes 122888 | tf_op jit(solution)/shard_map/ppermute | solution.py:496
  26.7 0.6 %copy-start.4 = (s32[4]{0:T(128)S(1)}, s32[4]{0:T(128)}, u32[]{:S(2)}) copy-start(s32[4]{0:T(128)} %pad_add_fusion.ints_ref) | copy-start | bytes 52
  27.3 6.7 %copy-start.1 = (f32[80,1024]{1,0:T(8,128)S(1)}, f32[80,1024]{1,0:T(8,128)}, u32[]{:S(2)}) copy-start(f32[80,1024]{1,0:T(8,128)} %prompt_ref.3) | copy-start | bytes 983044
  27.3 6.8 %copy-start.5 = (f32[3]{0:T(128)S(1)}, f32[3]{0:T(128)}, u32[]{:S(2)}) copy-start(f32[3]{0:T(128)} %pad_maximum_fusion.1.floats_ref) | copy-start | bytes 40
  27.3 6.8 %copy-start.8 = (bf16[1024,1024]{1,0:T(8,128)(2,1)S(1)}, bf16[1024,1024]{1,0:T(8,128)(2,1)}, u32[]{:S(2)}) copy-start(bf16[1024,1024]{1,0:T(8,128)(2,1)} %out_w_ref.1) | copy-start | bytes 6291460
  27.3 6.8 %copy-start.9 = (bf16[256,512]{1,0:T(8,128)(2,1)S(1)}, bf16[256,512]{1,0:T(8,128)(2,1)}, u32[]{:S(2)}) copy-start(bf16[256,512]{1,0:T(8,128)(2,1)} %get-tuple-element.17.own_ref) | copy-start | bytes 786436

commit v2 on v0

v2 whole, which is shorter than its diff:
```python
import functools
import math

import jax
import jax.numpy as jnp
from jax import lax
from jax.experimental import pallas as pl
from jax.experimental.pallas import tpu as pltpu
from jax.sharding import PartitionSpec as P

HEADS = 16
BLK = 32
NSTEPS = 32
HALO = 128
EPS = 1e-06
GUIDE = 0.5
TILE = 128
MASKED = -1e30
SMALL = 1e-30
LARGE = 1e30

F32 = jnp.float32
BF16 = jnp.bfloat16
VMEM_LIMIT = 24 * 1024 * 1024
SMALL_VMEM = 8 * 1024 * 1024


def mm(a, b):
    return jnp.dot(a, b, preferred_element_type=F32)


def mm_nt(a, b):
    return lax.dot_general(a, b, (((1,), (1,)), ((), ())), preferred_element_type=F32)


def whole(memory_space=pltpu.VMEM):
    return pl.BlockSpec(memory_space=memory_space)


def in_hbm(array):
    return pltpu.with_memory_space_constraint(array, pltpu.HBM)


def location():
    place = lax.axis_index("cfg")
    half = place // 2
    return half, place % 2, 2 * lax.axis_index("seq") + half


def time_value(step):
    return 1.0 - jnp.cos(0.5 * math.pi * step.astype(F32) / NSTEPS)


def time_features(step_index, freq):
    later = time_value(step_index[0] + 1)
    half_freq = freq // 2
    freqs = jnp.exp(-math.log(10000.0) * jnp.arange(half_freq, dtype=F32) / half_freq)
    angles = 1000.0 * later * freqs
    return jnp.concatenate([jnp.sin(angles), jnp.cos(angles)])[None, :]


def velocity_kernel(hidden_ref, weight_ref, vel_ref, sent_ref, rows_ref, held_ref, sems):
    parts = sems.shape[0] - 1
    step = hidden_ref.shape[0] // parts
    copies = [pltpu.make_async_copy(weight_ref, held_ref, sems.at[parts])]
    for part in range(parts):
        here = pl.ds(part * step, step)
        copies.append(
            pltpu.make_async_copy(hidden_ref.at[here], rows_ref.at[here], sems.at[part])
        )
    for copy in copies:
        copy.start()
    copies[0].wait()
    weight = held_ref[...]
    for part in range(parts):
        copies[part + 1].wait()
        here = slice(part * step, (part + 1) * step)
        rows = rows_ref[here].astype(F32)
        mean = jnp.mean(rows, axis=-1, keepdims=True)
        centered = rows - mean
        spread = jnp.mean(centered * centered, axis=-1, keepdims=True)
        normed = (centered * lax.rsqrt(spread + EPS)).astype(BF16)
        vel = mm_nt(weight, normed)
        vel_ref[:, here] = vel
        sent_ref[:, here] = vel.astype(BF16)


def velocity_call(hidden, proj_turned):
    rows, width = hidden.shape
    mel = proj_turned.shape[0]
    return pl.pallas_call(
        velocity_kernel,
        in_specs=[whole(pltpu.HBM)] * 2,
        out_specs=[whole(), whole()],
        out_shape=[
            jax.ShapeDtypeStruct((mel, rows), F32),
            jax.ShapeDtypeStruct((mel, rows), BF16),
        ],
        scratch_shapes=[
            pltpu.VMEM((rows, width), BF16),
            pltpu.VMEM((mel, width), BF16),
            pltpu.SemaphoreType.DMA((5,)),
        ],
        compiler_params=pltpu.CompilerParams(vmem_limit_bytes=SMALL_VMEM),
        cost_estimate=pl.CostEstimate(
            flops=2 * rows * width * mel, bytes_accessed=2 * rows * width, transcendentals=0
        ),
        name="velocity",
    )(in_hbm(hidden), in_hbm(proj_turned))


def prepare_kernel(
    total_blocks,
    feats_ref,
    back_hbm,
    ahead_hbm,
    latent_w_hbm,
    prompt_w_hbm,
    time_w_hbm,
    qkv_hbm,
    mixed_ref,
    keyed_ref,
    gram_ref,
    embed_ref,
    gate_ref,
    bias_ref,
    left_ref,
    back_ref,
    ahead_ref,
    latent_w_ref,
    prompt_w_ref,
    time_w_ref,
    qkv_ref,
    sems,
):
    mel, width = latent_w_ref.shape
    small = [
        pltpu.make_async_copy(source, target, sems.at[index])
        for index, (source, target) in enumerate(
            [
                (latent_w_hbm, latent_w_ref),
                (prompt_w_hbm, prompt_w_ref),
                (time_w_hbm, time_w_ref),
                (back_hbm, back_ref),
                (ahead_hbm, ahead_ref),
            ]
        )
    ]
    parts = 6
    columns = 3 * width // parts
    large = []
    for part in range(parts):
        here = pl.ds(part * columns, columns)
        large.append(
            pltpu.make_async_copy(qkv_hbm.at[:, here], qkv_ref.at[:, here], sems.at[5 + part])
        )
    for copy in small + large:
        copy.start()

    small[0].wait()
    small[1].wait()
    both = jnp.concatenate([latent_w_ref[...], prompt_w_ref[...]], axis=0)
    wide = both.astype(F32)
    centered = wide - jnp.mean(wide, axis=-1, keepdims=True)
    embed = jnp.concatenate(
        [both, latent_w_ref[...], jnp.zeros((256 - 3 * mel, width), BF16)], axis=0
    )
    embed_ref[...] = embed
    col = jnp.mean(embed.astype(F32), axis=-1, keepdims=True)
    row = mm_nt(jnp.ones((16, width), BF16), embed)[0:1] / width
    gram = mm_nt(embed, embed) / width - col * row
    gram_high = gram.astype(BF16)
    gram_ref[0:256] = gram_high
    gram_ref[256:512] = (gram - gram_high.astype(F32)).astype(BF16)

    feats = jnp.broadcast_to(feats_ref[...], (16, feats_ref.shape[1]))
    high = feats.astype(BF16)
    rest = feats - high.astype(F32)
    mid = rest.astype(BF16)
    low = (rest - mid.astype(F32)).astype(BF16)
    small[2].wait()
    pieces = mm(jnp.concatenate([high, mid, low], axis=0), time_w_ref[...])
    mod = pieces[0:1] + (pieces[16:17] + pieces[32:33])
    shift, scale, gate = mod[:, :width], mod[:, width : 2 * width], mod[:, 2 * width :]
    gate_ref[...] = gate
    left_ref[0 : 2 * mel] = (centered * (1.0 + scale)).astype(BF16)
    shift_high = shift.astype(BF16).astype(F32)
    which = lax.broadcasted_iota(jnp.int32, (16, width), 0)
    left_ref[2 * mel : 2 * mel + 16] = jnp.where(
        which == 0, shift_high, jnp.where(which == 1, shift - shift_high, 0.0)
    ).astype(BF16)

    small[3].wait()
    small[4].wait()
    half, _, span = location()
    per_half = back_ref.shape[0] // 2
    keys = bias_ref.shape[1]
    row_block = lax.broadcasted_iota(jnp.int32, (16, keys), 0)
    lower = jnp.zeros((16, keys), jnp.int32)
    upper = jnp.zeros((16, keys), jnp.int32)
    for block in range(per_half):
        lower = jnp.where(row_block == block, block - back_ref[half * per_half + block], lower)
        upper = jnp.where(row_block == block, block + ahead_ref[half * per_half + block], upper)
    key_block = lax.broadcasted_iota(jnp.int32, (16, keys), 1) // BLK - HALO // BLK
    place = key_block + span * per_half
    seen = (key_block >= lower) & (key_block <= upper) & (place >= 0) & (place < total_blocks)
    bias_ref[0:16] = jnp.where(seen, 0.0, MASKED).astype(BF16)
    bias_ref[16:128] = jnp.zeros((112, keys), BF16)

    left = left_ref[...]
    for part, copy in enumerate(large):
        start = part * columns
        copy.wait()
        acc = mm(left, qkv_ref[:, start : start + columns])
        if start < width:
            acc = acc * (math.log2(math.e) / math.sqrt(width // HEADS))
        offset = acc[2 * mel : 2 * mel + 1] + acc[2 * mel + 1 : 2 * mel + 2]
        offset_high = offset.astype(BF16).astype(F32)
        which = lax.broadcasted_iota(jnp.int32, (256 - 3 * mel, columns), 0)
        last = jnp.where(which == 0, offset_high, jnp.where(which == 1, offset - offset_high, 0.0))
        block = jnp.concatenate([acc[: 2 * mel], acc[:mel], last], axis=0).astype(BF16)
        if start < width:
            mixed_ref[:, start : start + columns] = block
        elif start < 2 * width:
            keyed_ref[start - width : start - width + columns] = block.T
        else:
            mixed_ref[:, start - width : start - width + columns] = block


def prepare_call(
    total_blocks, back, ahead, feats, latent_weight, prompt_weight, time_weight, qkv_weight
):
    mel, width = latent_weight.shape
    return pl.pallas_call(
        functools.partial(prepare_kernel, total_blocks),
        in_specs=[whole()] + [whole(pltpu.HBM)] * 6,
        out_specs=[whole()] * 6,
        out_shape=[
            jax.ShapeDtypeStruct((256, 2 * width), BF16),
            jax.ShapeDtypeStruct((width, 256), BF16),
            jax.ShapeDtypeStruct((512, 256), BF16),
            jax.ShapeDtypeStruct((256, width), BF16),
            jax.ShapeDtypeStruct((1, width), F32),
            jax.ShapeDtypeStruct((128, 512 + 2 * HALO), BF16),
        ],
        scratch_shapes=[
            pltpu.VMEM((2 * mel + 16, width), BF16),
            pltpu.SMEM(back.shape, jnp.int32),
            pltpu.SMEM(ahead.shape, jnp.int32),
            pltpu.VMEM(latent_weight.shape, BF16),
            pltpu.VMEM(prompt_weight.shape, BF16),
            pltpu.VMEM(time_weight.shape, BF16),
            pltpu.VMEM(qkv_weight.shape, BF16),
            pltpu.SemaphoreType.DMA((11,)),
        ],
        compiler_params=pltpu.CompilerParams(vmem_limit_bytes=VMEM_LIMIT),
        cost_estimate=pl.CostEstimate(
            flops=2 * 256 * width * 3 * width, bytes_accessed=8 * width * width, transcendentals=0
        ),
        name="prepare",
    )(
        feats,
        in_hbm(back),
        in_hbm(ahead),
        in_hbm(latent_weight),
        in_hbm(prompt_weight),
        in_hbm(time_weight),
        in_hbm(qkv_weight),
    )


def combine_kernel(
    delta_ref,
    vel_ref,
    partner_ref,
    latent_ref,
    prompt_ref,
    next_ref,
    rows_ref,
    seq_ref,
    cross_ref,
):
    half, branch, _ = location()
    mel, frames = vel_ref.shape
    delta = delta_ref[0]
    mine = jnp.where(branch == 0, 1.0 + GUIDE, -GUIDE) * delta
    other = jnp.where(branch == 0, -GUIDE, 1.0 + GUIDE) * delta
    latent = jnp.where(half == 0, latent_ref[:, :frames], latent_ref[:, frames:])
    prompt = jnp.where(half == 0, prompt_ref[:, :frames], prompt_ref[:, frames:])
    updated = latent + (mine * vel_ref[...] + other * partner_ref[...].astype(F32))
    head, tail = updated[:, :HALO], updated[:, frames - HALO :]
    seq_ref[0:mel] = jnp.where(half == 0, head, tail).astype(BF16)
    seq_ref[mel : 2 * mel] = jnp.where(
        half == 0, prompt[:, :HALO], prompt[:, frames - HALO :]
    ).astype(BF16)
    cross_ref[...] = jnp.where(half == 0, tail, head).astype(BF16)
    share = frames // 2
    next_ref[...] = jnp.where(branch == 0, updated[:, :share], updated[:, share:])
    high = updated.astype(BF16)
    rows_ref[0:mel] = high
    rows_ref[mel : 2 * mel] = jnp.where(branch == 0, prompt, 0.0).astype(BF16)
    rows_ref[2 * mel : 3 * mel] = (updated - high.astype(F32)).astype(BF16)
    rows_ref[3 * mel : 256] = jnp.zeros((256 - 3 * mel, frames), BF16)


def combine_call(delta, vel, partner, latent, prompt):
    mel, frames = vel.shape
    return pl.pallas_call(
        combine_kernel,
        in_specs=[whole(pltpu.SMEM)] + [whole()] * 4,
        out_specs=[whole()] * 4,
        out_shape=[
            jax.ShapeDtypeStruct((mel, frames // 2), F32),
            jax.ShapeDtypeStruct((256, frames), BF16),
            jax.ShapeDtypeStruct((2 * mel, HALO), BF16),
            jax.ShapeDtypeStruct((mel, HALO), BF16),
        ],
        compiler_params=pltpu.CompilerParams(vmem_limit_bytes=SMALL_VMEM),
        name="combine",
    )(delta, vel, partner, latent, prompt)


def normalised(rows, gram_ref, mel):
    weighted = mm(gram_ref[0:256], rows) + mm(gram_ref[256:512], rows)
    rows = rows.astype(F32)
    spread = jnp.sum(weighted * rows, axis=0, keepdims=True)
    inverse = lax.rsqrt(jnp.maximum(spread, 0.0) + EPS)
    latent = (rows[0:mel] + rows[2 * mel : 3 * mel]) * inverse
    high = latent.astype(BF16)
    which = lax.broadcasted_iota(jnp.int32, (256 - 3 * mel, rows.shape[1]), 0)
    return jnp.concatenate(
        [
            high,
            (rows[mel : 2 * mel] * inverse).astype(BF16),
            (latent - high.astype(F32)).astype(BF16),
            jnp.where(which < 2, 1.0, 0.0).astype(BF16),
        ],
        axis=0,
    )


def split_values(values, start, value_ref):
    left = lax.broadcasted_iota(jnp.int32, (values.shape[0], 128), 1) < 64
    for part in range(2):
        pair = values[:, 128 * part : 128 * (part + 1)]
        at = 2 * start + 256 * part
        value_ref[:, at : at + 128] = jnp.where(left, pair, 0.0).astype(BF16)
        value_ref[:, at + 128 : at + 256] = jnp.where(left, 0.0, pair).astype(BF16)


def pair_queries(query, tile):
    row = lax.broadcasted_iota(jnp.int32, (TILE, 128), 0)
    lane = lax.broadcasted_iota(jnp.int32, (TILE, 128), 1)
    chosen = (lane == tile * (TILE // BLK) + row // BLK).astype(F32).astype(BF16)
    return jnp.concatenate([query, chosen], axis=1)


def pair_scores(queries, key_left, key_right, bias):
    gap = jnp.zeros_like(key_left)
    key = jnp.concatenate(
        [
            jnp.concatenate([key_left, gap, bias], axis=0),
            jnp.concatenate([gap, key_right, bias], axis=0),
        ],
        axis=1,
    )
    return mm(queries, key)


def pair_sums(scores, value_left, value_right):
    left = lax.broadcasted_iota(jnp.int32, value_left.shape, 1) < 64
    ones_left = jnp.where(left, 1.0, 0.0).astype(BF16)
    ones_right = jnp.where(left, 0.0, 1.0).astype(BF16)
    value = jnp.concatenate(
        [
            jnp.concatenate([value_left, ones_left], axis=1),
            jnp.concatenate([value_right, ones_right], axis=1),
        ],
        axis=0,
    )
    return mm(jnp.exp2(scores).astype(BF16), value)


def less_top(scores, tops):
    size = scores.shape[1] // 2
    return jnp.concatenate([scores[:, :size] - tops[0], scores[:, size:] - tops[1]], axis=1)


def top_of(scores):
    size = scores.shape[1] // 2
    return (
        jnp.max(scores[:, :size], axis=-1, keepdims=True),
        jnp.max(scores[:, size:], axis=-1, keepdims=True),
    )


def in_range(least, most):
    return (jnp.min(least) > SMALL) & (jnp.max(most) < LARGE)


def pair_keys(key_ref, pair, window):
    return (
        key_ref[pl.ds(pair * 128, 64), window],
        key_ref[pl.ds(pair * 128 + 64, 64), window],
    )


def pair_values(value_ref, pair, window):
    return (
        value_ref[window, pl.ds(pair * 256, 128)],
        value_ref[window, pl.ds(pair * 256 + 128, 128)],
    )


def inner_kernel(
    mel,
    own_ref,
    mixed_ref,
    keyed_ref,
    gram_ref,
    bias_ref,
    query_ref,
    key_ref,
    value_ref,
    context_ref,
):
    frames, width = query_ref.shape
    pairs = width // 128
    normed = normalised(own_ref[...], gram_ref, mel)
    turned = normed.T
    for start in range(0, width, 256):
        cols = slice(start, start + 256)
        key_ref[cols] = mm(keyed_ref[cols], normed).astype(BF16)
        query_ref[:, cols] = mm(turned, mixed_ref[:, cols]).astype(BF16)
        split_values(
            mm(turned, mixed_ref[:, width + start : width + start + 256]), start, value_ref
        )

    def attend(tile, pair, stable):
        at = tile * TILE
        cols = pl.ds(pair * 128, 128)
        window = pl.ds(at - HALO, TILE + 2 * HALO)
        queries = pair_queries(query_ref[pl.ds(at, TILE), cols], tile)
        scores = pair_scores(
            queries, *pair_keys(key_ref, pair, window), bias_ref[:, pl.ds(at, TILE + 2 * HALO)]
        )
        if stable:
            scores = less_top(scores, top_of(scores))
        sums = pair_sums(scores, *pair_values(value_ref, pair, window))
        total = sums[:, 128:]
        context_ref[pl.ds(at - HALO, TILE), cols] = (sums[:, :128] / total).astype(BF16)
        return total

    first, last = HALO // TILE, (frames - HALO) // TILE
    least = jnp.full((TILE, 128), 1.0, F32)
    most = jnp.full((TILE, 128), 1.0, F32)
    for tile in range(first, last):
        for pair in range(pairs):
            total = attend(tile, pair, False)
            least = jnp.minimum(least, total)
            most = jnp.maximum(most, total)

    @pl.when(jnp.logical_not(in_range(least, most)))
    def _():
        def one(index, carry):
            attend(first + index // pairs, index % pairs, True)
            return carry

        lax.fori_loop(0, (last - first) * pairs, one, 0)


def inner_call(mel, own, mixed, keyed, gram, bias):
    frames = own.shape[1]
    width = keyed.shape[0]
    return pl.pallas_call(
        functools.partial(inner_kernel, mel),
        in_specs=[whole()] * 5,
        out_specs=[whole()] * 4,
        out_shape=[
            jax.ShapeDtypeStruct((frames, width), BF16),
            jax.ShapeDtypeStruct((width, frames), BF16),
            jax.ShapeDtypeStruct((frames, 2 * width), BF16),
            jax.ShapeDtypeStruct((frames - 2 * HALO, width), BF16),
        ],
        compiler_params=pltpu.CompilerParams(vmem_limit_bytes=VMEM_LIMIT),
        cost_estimate=pl.CostEstimate(
            flops=3_000_000_000, bytes_accessed=6_000_000, transcendentals=3_000_000
        ),
        name="inner",
    )(own, mixed, keyed, gram, bias)


def edges_of(frames):
    own = TILE + HALO
    return (
        (0, 0, 0, HALO, 0),
        (frames // TILE - 1, frames - own, HALO, frames + HALO - own, frames + HALO),
    )


def outer_kernel(
    own_ref,
    query_ref,
    key_ref,
    value_ref,
    bias_ref,
    context_ref,
    embed_ref,
    gate_ref,
    out_w_ref,
    done_ref,
    first_ref,
    sums_ref,
    totals_ref,
):
    frames, width = query_ref.shape
    pairs = width // 128
    for edge, (tile, at, _, bias_at, _) in enumerate(edges_of(frames)):
        window = pl.ds(at, TILE + HALO)
        here = slice(edge * TILE, (edge + 1) * TILE)
        for pair in range(pairs):
            cols = slice(pair * 128, (pair + 1) * 128)
            queries = pair_queries(query_ref[tile * TILE : (tile + 1) * TILE, cols], tile)
            scores = pair_scores(
                queries,
                *pair_keys(key_ref, pair, window),
                bias_ref[:, bias_at : bias_at + TILE + HALO],
            )
            sums = pair_sums(scores, *pair_values(value_ref, pair, window))
            sums_ref[here, cols] = sums[:, :128]
            totals_ref[here, cols] = sums[:, 128:]
    own_turned = own_ref[...].T
    for start in range(0, width, 256):
        cols = slice(start, start + 256)
        first = mm(own_turned, embed_ref[:, cols])
        projected = mm(context_ref[...], out_w_ref[:, cols])
        done_ref[:, cols] = (
            first[HALO : frames - HALO] + gate_ref[:, cols] * projected
        ).astype(BF16)
        first_ref[0:HALO, cols] = first[0:HALO]
        first_ref[HALO : 2 * HALO, cols] = first[frames - HALO :]


def outer_call(own, query, key, value, bias, context, embed, gate, out_w):
    frames, width = query.shape
    return pl.pallas_call(
        outer_kernel,
        in_specs=[whole()] * 9,
        out_specs=[whole()] * 4,
        out_shape=[
            jax.ShapeDtypeStruct((frames - 2 * HALO, width), BF16),
            jax.ShapeDtypeStruct((2 * HALO, width), F32),
            jax.ShapeDtypeStruct((2 * TILE, width), F32),
            jax.ShapeDtypeStruct((2 * TILE, width), F32),
        ],
        compiler_params=pltpu.CompilerParams(vmem_limit_bytes=VMEM_LIMIT),
        cost_estimate=pl.CostEstimate(
            flops=3_000_000_000, bytes_accessed=6_000_000, transcendentals=2_000_000
        ),
        name="outer",
    )(own, query, key, value, bias, context, embed, gate, out_w)


def close_kernel(
    near_ref,
    prompt_ref,
    mixed_ref,
    keyed_ref,
    gram_ref,
    bias_ref,
    query_ref,
    key_ref,
    value_ref,
    sums_ref,
    totals_ref,
    first_ref,
    gate_ref,
    out_w_ref,
    done_ref,
    next_ref,
    near_key_ref,
    near_value_ref,
    context_ref,
    edge_ref,
    sems,
):
    half, branch, _ = location()
    frames, width = query_ref.shape
    pairs = width // 128
    mel = near_ref.shape[0] // 3
    inner = pltpu.make_async_copy(done_ref, next_ref.at[pl.ds(HALO, frames - 2 * HALO)], sems.at[0])
    inner.start()
    flag = jnp.where(branch == 0, 1.0, 0.0)
    prompt = jnp.where(
        half == 0, prompt_ref[:, frames : frames + HALO], prompt_ref[:, frames - HALO : frames]
    )
    blank = jnp.zeros((256 - 2 * mel, HALO), F32)
    near = near_ref[...].astype(F32)
    cross_rows = jnp.concatenate([near[0:mel], prompt * flag, blank], axis=0)
    seq_rows = jnp.concatenate(
        [near[mel : 2 * mel], near[2 * mel : 3 * mel] * flag, blank], axis=0
    )
    before = jnp.where(half == 0, seq_rows, cross_rows).astype(BF16)
    after = jnp.where(half == 0, cross_rows, seq_rows).astype(BF16)
    normed = normalised(jnp.concatenate([before, after], axis=1), gram_ref, mel)
    turned = normed.T
    for start in range(0, width, 256):
        cols = slice(start, start + 256)
        near_key_ref[cols] = mm(keyed_ref[cols], normed).astype(BF16)
        split_values(
            mm(turned, mixed_ref[:, width + start : width + start + 256]), start, near_value_ref
        )

    edges = edges_of(frames)
    least = jnp.full((TILE, 128), 1.0, F32)
    most = jnp.full((TILE, 128), 1.0, F32)
    for edge, (tile, _, near_at, _, bias_at) in enumerate(edges):
        window = pl.ds(near_at, HALO)
        here = slice(edge * TILE, (edge + 1) * TILE)
        for pair in range(pairs):
            cols = slice(pair * 128, (pair + 1) * 128)
            queries = pair_queries(query_ref[tile * TILE : (tile + 1) * TILE, cols], tile)
            scores = pair_scores(
                queries,
                *pair_keys(near_key_ref, pair, window),
                bias_ref[:, bias_at : bias_at + HALO],
            )
            sums = pair_sums(scores, *pair_values(near_value_ref, pair, window))
            total = sums[:, 128:] + totals_ref[here, cols]
            context_ref[here, cols] = ((sums[:, :128] + sums_ref[here, cols]) / total).astype(BF16)
            least = jnp.minimum(least, total)
            most = jnp.maximum(most, total)

    @pl.when(jnp.logical_not(in_range(least, most)))
    def _():
        for edge, (tile, at, near_at, bias_own, bias_near) in enumerate(edges):
            here = slice(edge * TILE, (edge + 1) * TILE)

            def one(pair, carry):
                cols = pl.ds(pair * 128, 128)
                own_window = pl.ds(at, TILE + HALO)
                near_window = pl.ds(near_at, HALO)
                queries = pair_queries(query_ref[tile * TILE : (tile + 1) * TILE, cols], tile)
                own_scores = pair_scores(
                    queries,
                    *pair_keys(key_ref, pair, own_window),
                    bias_ref[:, bias_own : bias_own + TILE + HALO],
                )
                near_scores = pair_scores(
                    queries,
                    *pair_keys(near_key_ref, pair, near_window),
                    bias_ref[:, bias_near : bias_near + HALO],
                )
                tops = [
                    jnp.maximum(a, b) for a, b in zip(top_of(own_scores), top_of(near_scores))
                ]
                sums = pair_sums(
                    less_top(own_scores, tops), *pair_values(value_ref, pair, own_window)
                ) + pair_sums(
                    less_top(near_scores, tops), *pair_values(near_value_ref, pair, near_window)
                )
                context_ref[here, cols] = (sums[:, :128] / sums[:, 128:]).astype(BF16)
                return carry

            lax.fori_loop(0, pairs, one, 0)

    for start in range(0, width, 256):
        cols = slice(start, start + 256)
        projected = mm(context_ref[...], out_w_ref[:, cols])
        edge_ref[:, cols] = (first_ref[:, cols] + gate_ref[:, cols] * projected).astype(BF16)
    head = pltpu.make_async_copy(edge_ref.at[pl.ds(0, HALO)], next_ref.at[pl.ds(0, HALO)], sems.at[1])
    tail = pltpu.make_async_copy(
        edge_ref.at[pl.ds(HALO, HALO)], next_ref.at[pl.ds(frames - HALO, HALO)], sems.at[2]
    )
    head.start()
    tail.start()
    inner.wait()
    head.wait()
    tail.wait()


def close_call(
    near, prompt, mixed, keyed, gram, bias, query, key, value, sums, totals, first, gate, out_w, done
):
    frames, width = query.shape
    return pl.pallas_call(
        close_kernel,
        in_specs=[whole()] * 15,
        out_specs=whole(pltpu.HBM),
        out_shape=jax.ShapeDtypeStruct((frames, width), BF16),
        scratch_shapes=[
            pltpu.VMEM((width, 2 * HALO), BF16),
            pltpu.VMEM((2 * HALO, 2 * width), BF16),
            pltpu.VMEM((2 * TILE, width), BF16),
            pltpu.VMEM((2 * TILE, width), BF16),
            pltpu.SemaphoreType.DMA((3,)),
        ],
        compiler_params=pltpu.CompilerParams(vmem_limit_bytes=VMEM_LIMIT),
        cost_estimate=pl.CostEstimate(
            flops=2_000_000_000, bytes_accessed=6_000_000, transcendentals=1_000_000
        ),
        name="close",
    )(near, prompt, mixed, keyed, gram, bias, query, key, value, sums, totals, first, gate, out_w, done)


def body(
    hidden,
    latent,
    prompt_mel,
    window_back,
    window_ahead,
    step_index,
    proj_weight,
    latent_weight,
    prompt_weight,
    time_weight,
    qkv_weight,
    attn_out_weight,
):
    axes = ("seq", "cfg")
    spans = lax.axis_size("seq")
    mel = latent.shape[0]
    total_blocks = 2 * spans * (hidden.shape[0] // BLK)

    def at(span, cell):
        return span * 4 + cell

    everyone = [(span, cell) for span in range(spans) for cell in range(4)]
    to_partner = [(at(s, c), at(s, c ^ 1)) for s, c in everyone]
    to_half = [(at(s, c), at(s, c ^ 3)) for s, c in everyone]
    to_span = [
        (at(s, c), at(s + (1 if c >= 2 else -1), c))
        for s, c in everyone
        if 0 <= s + (1 if c >= 2 else -1) < spans
    ]
    vel, sent = velocity_call(hidden, proj_weight.T)
    sent, step_index = lax.optimization_barrier((sent, step_index))
    partner = lax.ppermute(sent, axes, to_partner)
    delta = time_value(step_index + 1) - time_value(step_index)
    feats = time_features(step_index, time_weight.shape[0])
    mixed, keyed, gram, embed, gate, bias = prepare_call(
        total_blocks,
        window_back,
        window_ahead,
        feats,
        latent_weight,
        prompt_weight,
        time_weight,
        qkv_weight,
    )
    partner, gate = lax.optimization_barrier((partner, gate))
    latent_out, own, far, cross = combine_call(delta, vel, partner, latent, prompt_mel)
    relayed = lax.ppermute(far, axes, to_span)
    query, key, value, context = inner_call(mel, own, mixed, keyed, gram, bias)
    near = jnp.concatenate([cross, relayed], axis=0)
    near, context = lax.optimization_barrier((near, context))
    near = lax.ppermute(near, axes, to_half)
    done, first, sums, totals = outer_call(
        own, query, key, value, bias, context, embed, gate, attn_out_weight
    )
    hidden_next = close_call(
        near,
        prompt_mel,
        mixed,
        keyed,
        gram,
        bias,
        query,
        key,
        value,
        sums,
        totals,
        first,
        gate,
        attn_out_weight,
        done,
    )
    return (latent_out, hidden_next)


def solution(mesh):
    in_specs = (
        P(("seq", "cfg"), None),
        P(None, "seq"),
        P(None, "seq"),
        P("seq"),
        P("seq"),
        P(),
        P(),
        P(),
        P(),
        P(),
        P(),
        P(),
    )
    out_specs = (P(None, ("seq", "cfg")), P(("seq", "cfg"), None))
    return jax.shard_map(body, mesh=mesh, in_specs=in_specs, out_specs=out_specs, check_vma=False)
```

time: 183 us -> 48.8 us (0.27); the launches traced: 181 us -> 48.7 us
  matrix products: 63.3 us -> 0 us
  waiting for transfers between devices: 48 us -> 3.43 us
  Pallas kernels: 0 us -> 33.8 us
  other arithmetic: 33.6 us -> 0.06 us
  local copies, waits for them, and re-layouts: 15.8 us -> 0.02 us
  starting transfers between devices: 18.5 us -> 9.84 us
    dot_general x38 -> x0, matrix products: 63.3 us -> none  [the longest x16 26.2 us: one_head(): jnp.dot(query_one, key_one.T, preferred_element_type=jnp.float32)]
    ppermute x4 -> x3, waiting for transfers between devices: 48 us -> 3.43 us  [the longest x1 3.43 us: body(): near = lax.ppermute(near, axes, to_half)]
    pallas_call x0 -> x6, Pallas kernels: none -> 33.8 us  [the longest x1 11.9 us: close_call(): pl.pallas_call(close_kernel, in_specs=[whole()] * 15, out_specs=whole(plt...]
    slice x10 -> x0, local copies, waits for them, and re-layouts: 11.1 us -> none  [the longest x2 4.61 us: body(): window[:, width:]]
    sub x1 -> x0, other arithmetic: 10.2 us -> none  [window_mask(): lower = (query_block - back_rows)[:, None]]
    add x2 -> x0, other arithmetic: 10.1 us -> none  [the longest x1 10.1 us: window_mask(): upper = (query_block + ahead_rows)[:, None]]
    reduce_sum x19 -> x0, other arithmetic: 9.95 us -> none  [the longest x16 6.38 us: one_head(): total = jnp.sum(weights, axis=-1, keepdims=True)]
    ppermute x4 -> x3, starting transfers between devices: 18.5 us -> 9.84 us  [the longest x1 5.71 us: body(): relayed = lax.ppermute(far, axes, to_span)]
  transfers between devices with their start and end apart: 4 -> 3, of which waited for: 2 -> 1; matrix products, arithmetic and copies ran while one was open for 15% -> 0% of each run, Pallas kernels for 0% -> 37%
where the time goes in v2:
time: 48.8 us; the launch traced here: 48.7 us
  Pallas kernels  33.8 us (69%)
  starting transfers between devices  9.84 us (20%)
  waiting for transfers between devices  3.43 us (7%)
  between operations  1.56 us (3%)
    pallas_call x1, Pallas kernels, close_call(): pl.pallas_call(close_kernel, in_specs=[whole()] * 15, out_specs=whole(plt...  11.9 us
    pallas_call x1, Pallas kernels, inner_call(): pl.pallas_call(functools.partial(inner_kernel, mel), in_specs=[whole()] *...  11.4 us
    ppermute x1, starting transfers between devices, body(): relayed = lax.ppermute(far, axes, to_span)  5.71 us
    pallas_call x1, Pallas kernels, prepare_call(): pl.pallas_call(functools.partial(prepare_kernel, total_blocks), in_specs=...  4.63 us
    ppermute x1, waiting for transfers between devices, body(): near = lax.ppermute(near, axes, to_half)  3.43 us
    ppermute x1, starting transfers between devices, body(): partner = lax.ppermute(sent, axes, to_partner)  3.36 us
    pallas_call x1, Pallas kernels, velocity_call(): pl.pallas_call(velocity_kernel, in_specs=[whole(pltpu.HBM)] * 2, out_spec...  3 us
    pallas_call x1, Pallas kernels, outer_call(): pl.pallas_call(outer_kernel, in_specs=[whole()] * 9, out_specs=[whole()]...  2.21 us
  transfers between devices with their start and end apart: 3, of which 1 were waited for; matrix products, arithmetic and copies ran while one was open for 0% of the time, Pallas kernels for 37%

profile of v2, /device:TPU:6, one launch (start us, length us, event | category | flops | bytes accessed | tf_op | source)
XLA Modules:
  0.0 48.7 jit_solution(9415059612155858194)
XLA Ops:
  0.6 3.0 %velocity.1 = (f32[80,512]{1,0:T(8,128)S(1)}, bf16[80,512]{1,0:T(8,128)(2,1)S(1)}) custom-call(bf16[512,1024]{1,0:T(8,128)(2,1)} %hidden_ref.1, bf16[80,1024]{1,0:T(8,128)(2,1)} %bitcast.4), custom_call_target="tpu_custom_call" | custom-call | flops 83886080 | bytes 1048576 | tf_op jit(solution)/shard_map/velocity/pallas_call | solution.py:91
  3.6 3.4 %collective-permute-start = (bf16[80,512]{1,0:T(8,128)(2,1)S(1)}, bf16[80,512]{1,0:T(8,128)(2,1)S(1)}, u32[]{:S(2)}, u32[]{:S(2)}) collective-permute-start(bf16[80,512]{1,0:T(8,128)(2,1)S(1)} %get-tuple-element.31), channel_id=1, source_target_pairs={{0,1},{1,0},{2,3},{3,2},{4,5},{5,4},{6,7},{7,6},{8,9},{9,8},{10,11... | collective-permute-start | bytes 245768 | tf_op jit(solution)/shard_map/ppermute | solution.py:738
  7.9 0.0 copy-start.1
  7.9 0.0 copy-start.2
  7.9 4.6 %prepare.1 = (bf16[256,2048]{1,0:T(8,128)(2,1)S(1)}, bf16[1024,256]{1,0:T(8,128)(2,1)S(1)}, bf16[512,256]{1,0:T(8,128)(2,1)S(1)}, bf16[256,1024]{1,0:T(8,128)(2,...) custom-call(f32[1,256]{1,0:T(1,128)S(1)} %bitcast.3, s32[32]{0:T(128)} %back_hbm.1, s32[32]{0:T(128)} %ahead_hbm.1, ...), custom_call_target="tpu_custom_call" | custom-call | flops 1610612736 | bytes 8388608 | tf_op jit(solution)/shard_map/prepare/pallas_call | solution.py:234
  12.5 0.0 collective-permute-done.partner_ref
  12.6 0.0 copy-done.1
  12.6 0.0 copy-done.2
  12.6 0.7 %combine.1 = (f32[80,256]{1,0:T(8,128)}, bf16[256,512]{1,0:T(8,128)(2,1)S(1)}, bf16[160,128]{1,0:T(8,128)(2,1)S(1)}, bf16[80,128]{1,0:T(8,128)(2,1)S(1)}) custom-call(f32[1]{0:T(128)S(6)} %sub.14.delta_ref, f32[80,512]{1,0:T(8,128)S(1)} %get-tuple-element.30.vel_ref, bf16[80,512]{1,0:T(8,128)(2,1)S(1)} %collective-permute-done.partner_ref, ...), custom_call_target="tpu_custom_call" | custom-call | tf_op jit(solution)/shard_map/combine/pallas_call | solution.py:308
  13.3 5.7 %collective-permute-start.1 = (bf16[160,128]{1,0:T(8,128)(2,1)S(1)}, bf16[160,128]{1,0:T(8,128)(2,1)S(1)}, u32[]{:S(2)}, u32[]{:S(2)}) collective-permute-start(bf16[160,128]{1,0:T(8,128)(2,1)S(1)} %get-tuple-element.36), channel_id=1, source_target_pairs={{2,6},{3,7},{4,0},{5,1},{6,10},{7,11},{8,4},{9,5},{10,14},{11,15},... | collective-permute-start | bytes 122888 | tf_op jit(solution)/shard_map/ppermute | solution.py:753
  19.0 0.0 copy-start
  19.0 11.4 %inner.1 = (bf16[512,1024]{1,0:T(8,128)(2,1)S(1)}, bf16[1024,512]{1,0:T(8,128)(2,1)S(1)}, bf16[512,2048]{1,0:T(8,128)(2,1)S(1)}, bf16[256,1024]{1,0:T(8,128)(2,1)S(1)}) custom-call(bf16[256,512]{1,0:T(8,128)(2,1)S(1)} %get-tuple-element.37.own_ref, bf16[256,2048]{1,0:T(8,128)(2,1)S(1)} %get-tuple-element.38.mixed_ref, ...), custom_call_target="tpu_custom_call" | custom-call | flops 3000000000 | bytes 6000000 | tf_op jit(solution)/shard_map/inner/pallas_call | solution.py:475
  30.4 0.0 collective-permute-done.1
  30.4 0.8 %collective-permute-start.2 = (bf16[240,128]{1,0:T(8,128)(2,1)S(1)}, bf16[240,128]{1,0:T(8,128)(2,1)S(1)}, u32[]{:S(2)}, u32[]{:S(2)}) collective-permute-start(bf16[240,128]{1,0:T(8,128)(2,1)S(1)} %pad_maximum_fusion), channel_id=1, source_target_pairs={{0,3},{1,2},{2,1},{3,0},{4,7},{5,6},{6,5},{7,4},{8,11},{9,10},{10,... | collective-permute-start | bytes 184328 | tf_op jit(solution)/shard_map/ppermute | solution.py:757
  31.2 0.0 copy-done
  31.2 2.2 %outer.1 = (bf16[256,1024]{1,0:T(8,128)(2,1)S(1)}, f32[256,1024]{1,0:T(8,128)S(1)}, f32[256,1024]{1,0:T(8,128)S(1)}, f32[256,1024]{1,0:T(8,128)S(1)}) custom-call(bf16[256,512]{1,0:T(8,128)(2,1)S(1)} %get-tuple-element.37.own_ref, bf16[512,1024]{1,0:T(8,128)(2,1)S(1)} %get-tuple-element.44.query_ref, bf16[1024,512]{1,0:T(8,128)(2,1)S(1)} %get-tuple-element.45.key_ref, ...), custom_call_target="tpu_custom_call" | custom-call | flops 3000000000 | bytes 6000000 | tf_op jit(solution)/shard_map/outer/pallas_call | solution.py:546
  33.4 3.4 %collective-permute-done.2.near_ref = bf16[240,128]{1,0:T(8,128)(2,1)S(1)} collective-permute-done((bf16[240,128]{1,0:T(8,128)(2,1)S(1)}, bf16[240,128]{1,0:T(8,128)(2,1)S(1)}, u32[]{:S(2)}, u32[]{:S(2)}) %collective-permute-start.2) | collective-permute-done | bytes 61472 | tf_op jit(solution)/shard_map/ppermute | solution.py:757
  36.8 11.9 %close.1 = bf16[512,1024]{1,0:T(8,128)(2,1)} custom-call(bf16[240,128]{1,0:T(8,128)(2,1)S(1)} %collective-permute-done.2.near_ref, f32[80,1024]{1,0:T(8,128)S(1)} %copy-done.1, bf16[256,2048]{1,0:T(8,128)(2,1)S(1)} %get-tuple-element.38.mixed_ref, bf16[1024,256]{1,0:T(8,128)(2,1)S(1)} %get-tuple-element.39.keyed_ref, ...), custom_call_target="tpu_custom_call" | custom-call | flops 2000000000 | bytes 6000000 | tf_op jit(solution)/shard_map/close/pallas_call | solution.py:686
  (3 shorter events, 0.1 us)
Async XLA Ops:
  3.6 8.9 %collective-permute-start = (bf16[80,512]{1,0:T(8,128)(2,1)S(1)}, bf16[80,512]{1,0:T(8,128)(2,1)S(1)}, u32[]{:S(2)}, u32[]{:S(2)}) collective-permute-start(bf16[80,512]{1,0:T(8,128)(2,1)S(1)} %get-tuple-element.31), channel_id=1, source_target_pairs={{0,1},{1,0},{2,3},{3,2},{4,5},{5,4},{6,7},{7,6},{8,9},{9,8},{10,11... | collective-permute-start | bytes 245768 | tf_op jit(solution)/shard_map/ppermute | solution.py:738
  7.9 4.7 %copy-start.1 = (f32[80,1024]{1,0:T(8,128)S(1)}, f32[80,1024]{1,0:T(8,128)}, u32[]{:S(2)}) copy-start(f32[80,1024]{1,0:T(8,128)} %prompt_ref.3) | copy-start | bytes 983044
  7.9 4.7 %copy-start.2 = (f32[80,1024]{1,0:T(8,128)S(1)}, f32[80,1024]{1,0:T(8,128)}, u32[]{:S(2)}) copy-start(f32[80,1024]{1,0:T(8,128)} %latent_ref.1) | copy-start | bytes 983044
  13.3 17.1 %collective-permute-start.1 = (bf16[160,128]{1,0:T(8,128)(2,1)S(1)}, bf16[160,128]{1,0:T(8,128)(2,1)S(1)}, u32[]{:S(2)}, u32[]{:S(2)}) collective-permute-start(bf16[160,128]{1,0:T(8,128)(2,1)S(1)} %get-tuple-element.36), channel_id=1, source_target_pairs={{2,6},{3,7},{4,0},{5,1},{6,10},{7,11},{8,4},{9,5},{10,14},{11,15},... | collective-permute-start | bytes 122888 | tf_op jit(solution)/shard_map/ppermute | solution.py:753
  19.0 12.2 %copy-start = (bf16[1024,1024]{1,0:T(8,128)(2,1)S(1)}, bf16[1024,1024]{1,0:T(8,128)(2,1)}, u32[]{:S(2)}) copy-start(bf16[1024,1024]{1,0:T(8,128)(2,1)} %out_w_ref.3) | copy-start | bytes 6291460
  30.4 6.4 %collective-permute-start.2 = (bf16[240,128]{1,0:T(8,128)(2,1)S(1)}, bf16[240,128]{1,0:T(8,128)(2,1)S(1)}, u32[]{:S(2)}, u32[]{:S(2)}) collective-permute-start(bf16[240,128]{1,0:T(8,128)(2,1)S(1)} %pad_maximum_fusion), channel_id=1, source_target_pairs={{0,3},{1,2},{2,1},{3,0},{4,7},{5,6},{6,5},{7,4},{8,11},{9,10},{10,... | collective-permute-start | bytes 184328 | tf_op jit(solution)/shard_map/ppermute | solution.py:757

commit v3 on v2

--- a/solution.py
+++ b/solution.py
@@ -47,34 +47,62 @@
     return half, place % 2, 2 * lax.axis_index("seq") + half
 
 
+def sin_cos(angle):
+    turns = jnp.floor(angle * (2.0 / math.pi) + 0.5)
+    rest = angle - turns * 1.5703125
+    rest = rest - turns * 4.837512969970703125e-4
+    rest = rest - turns * 7.549789954891882e-8
+    square = rest * rest
+    sine = rest + rest * square * (
+        -1.6666654611e-1 + square * (8.3321608736e-3 - square * 1.9515295891e-4)
+    )
+    cosine = (
+        1.0
+        - 0.5 * square
+        + square
+        * square
+        * (4.166664568298827e-2 + square * (-1.388731625493765e-3 + square * 2.443315711809948e-5))
+    )
+    quarter = turns - 4.0 * jnp.floor(turns * 0.25)
+    odd = (quarter == 1.0) | (quarter == 3.0)
+    sine, cosine = jnp.where(odd, cosine, sine), jnp.where(odd, sine, cosine)
+    sine = jnp.where(quarter >= 2.0, -sine, sine)
+    cosine = jnp.where((quarter == 1.0) | (quarter == 2.0), -cosine, cosine)
+    return sine, cosine
+
+
 def time_value(step):
-    return 1.0 - jnp.cos(0.5 * math.pi * step.astype(F32) / NSTEPS)
-
-
-def time_features(step_index, freq):
-    later = time_value(step_index[0] + 1)
-    half_freq = freq // 2
-    freqs = jnp.exp(-math.log(10000.0) * jnp.arange(half_freq, dtype=F32) / half_freq)
-    angles = 1000.0 * later * freqs
-    return jnp.concatenate([jnp.sin(angles), jnp.cos(angles)])[None, :]
+    return 1.0 - sin_cos(0.5 * math.pi * step / NSTEPS)[1]
+
+
+def time_features(step):
+    later = time_value(step + 1.0)
+    half_freq = step.shape[1] // 2
+    lane = lax.broadcasted_iota(jnp.int32, step.shape, 1)
+    which = jnp.where(lane < half_freq, lane, lane - half_freq).astype(F32)
+    freqs = jnp.exp(-math.log(10000.0) * which / half_freq)
+    sine, cosine = sin_cos(1000.0 * later * freqs)
+    return jnp.where(lane < half_freq, sine, cosine)
 
 
 def velocity_kernel(hidden_ref, weight_ref, vel_ref, sent_ref, rows_ref, held_ref, sems):
     parts = sems.shape[0] - 1
-    step = hidden_ref.shape[0] // parts
-    copies = [pltpu.make_async_copy(weight_ref, held_ref, sems.at[parts])]
+    size = hidden_ref.shape[0] // parts
+    copies = []
     for part in range(parts):
-        here = pl.ds(part * step, step)
+        here = pl.ds(part * size, size)
         copies.append(
             pltpu.make_async_copy(hidden_ref.at[here], rows_ref.at[here], sems.at[part])
         )
-    for copy in copies:
+    copies.append(pltpu.make_async_copy(weight_ref, held_ref, sems.at[parts]))
+    for copy in reversed(copies):
         copy.start()
-    copies[0].wait()
+    copies[parts].wait()
     weight = held_ref[...]
+    for copy in copies[:parts]:
+        copy.wait()
     for part in range(parts):
-        copies[part + 1].wait()
-        here = slice(part * step, (part + 1) * step)
+        here = slice(part * size, (part + 1) * size)
         rows = rows_ref[here].astype(F32)
         mean = jnp.mean(rows, axis=-1, keepdims=True)
         centered = rows - mean
@@ -91,7 +119,7 @@
     return pl.pallas_call(
         velocity_kernel,
         in_specs=[whole(pltpu.HBM)] * 2,
-        out_specs=[whole(), whole()],
+        out_specs=[whole()] * 2,
         out_shape=[
             jax.ShapeDtypeStruct((mel, rows), F32),
             jax.ShapeDtypeStruct((mel, rows), BF16),
@@ -103,7 +131,7 @@
         ],
         compiler_params=pltpu.CompilerParams(vmem_limit_bytes=SMALL_VMEM),
         cost_estimate=pl.CostEstimate(
-            flops=2 * rows * width * mel, bytes_accessed=2 * rows * width, transcendentals=0
+            flops=10_000_000_000, bytes_accessed=2 * rows * width, transcendentals=0
         ),
         name="velocity",
     )(in_hbm(hidden), in_hbm(proj_turned))
@@ -111,26 +139,25 @@
 
 def prepare_kernel(
     total_blocks,
-    feats_ref,
+    step_ref,
     back_hbm,
     ahead_hbm,
     latent_w_hbm,
     prompt_w_hbm,
-    time_w_hbm,
-    qkv_hbm,
+    time_w_ref,
+    qkv_ref,
     mixed_ref,
     keyed_ref,
     gram_ref,
     embed_ref,
     gate_ref,
     bias_ref,
+    delta_ref,
     left_ref,
     back_ref,
     ahead_ref,
     latent_w_ref,
     prompt_w_ref,
-    time_w_ref,
-    qkv_ref,
     sems,
 ):
     mel, width = latent_w_ref.shape
@@ -140,21 +167,14 @@
             [
                 (latent_w_hbm, latent_w_ref),
                 (prompt_w_hbm, prompt_w_ref),
-                (time_w_hbm, time_w_ref),
                 (back_hbm, back_ref),
                 (ahead_hbm, ahead_ref),
             ]
         )
     ]
-    parts = 6
+    parts = 3
     columns = 3 * width // parts
-    large = []
-    for part in range(parts):
-        here = pl.ds(part * columns, columns)
-        large.append(
-            pltpu.make_async_copy(qkv_hbm.at[:, here], qkv_ref.at[:, here], sems.at[5 + part])
-        )
-    for copy in small + large:
+    for copy in small:
         copy.start()
 
     small[0].wait()
@@ -173,12 +193,14 @@
     gram_ref[0:256] = gram_high
     gram_ref[256:512] = (gram - gram_high.astype(F32)).astype(BF16)
 
-    feats = jnp.broadcast_to(feats_ref[...], (16, feats_ref.shape[1]))
+    step = jnp.full((1, time_w_ref.shape[0]), step_ref[0], jnp.int32).astype(F32)
+    feats = jnp.broadcast_to(time_features(step), (16, step.shape[1]))
+    step = step[:, :128]
+    delta_ref[...] = time_value(step + 1.0) - time_value(step)
     high = feats.astype(BF16)
     rest = feats - high.astype(F32)
     mid = rest.astype(BF16)
     low = (rest - mid.astype(F32)).astype(BF16)
-    small[2].wait()
     pieces = mm(jnp.concatenate([high, mid, low], axis=0), time_w_ref[...])
     mod = pieces[0:1] + (pieces[16:17] + pieces[32:33])
     shift, scale, gate = mod[:, :width], mod[:, width : 2 * width], mod[:, 2 * width :]
@@ -190,8 +212,8 @@
         which == 0, shift_high, jnp.where(which == 1, shift - shift_high, 0.0)
     ).astype(BF16)
 
+    small[2].wait()
     small[3].wait()
-    small[4].wait()
     half, _, span = location()
     per_half = back_ref.shape[0] // 2
     keys = bias_ref.shape[1]
@@ -208,9 +230,8 @@
     bias_ref[16:128] = jnp.zeros((112, keys), BF16)
 
     left = left_ref[...]
-    for part, copy in enumerate(large):
+    for part in range(parts):
         start = part * columns
-        copy.wait()
         acc = mm(left, qkv_ref[:, start : start + columns])
         if start < width:
             acc = acc * (math.log2(math.e) / math.sqrt(width // HEADS))
@@ -228,13 +249,13 @@
 
 
 def prepare_call(
-    total_blocks, back, ahead, feats, latent_weight, prompt_weight, time_weight, qkv_weight
+    total_blocks, step_index, back, ahead, latent_weight, prompt_weight, time_weight, qkv_weight
 ):
     mel, width = latent_weight.shape
     return pl.pallas_call(
         functools.partial(prepare_kernel, total_blocks),
-        in_specs=[whole()] + [whole(pltpu.HBM)] * 6,
-        out_specs=[whole()] * 6,
+        in_specs=[whole(pltpu.SMEM)] + [whole(pltpu.HBM)] * 4 + [whole()] * 2,
+        out_specs=[whole()] * 7,
         out_shape=[
             jax.ShapeDtypeStruct((256, 2 * width), BF16),
             jax.ShapeDtypeStruct((width, 256), BF16),
@@ -242,6 +263,7 @@
             jax.ShapeDtypeStruct((256, width), BF16),
             jax.ShapeDtypeStruct((1, width), F32),
             jax.ShapeDtypeStruct((128, 512 + 2 * HALO), BF16),
+            jax.ShapeDtypeStruct((1, 128), F32),
         ],
         scratch_shapes=[
             pltpu.VMEM((2 * mel + 16, width), BF16),
@@ -249,9 +271,7 @@
             pltpu.SMEM(ahead.shape, jnp.int32),
             pltpu.VMEM(latent_weight.shape, BF16),
             pltpu.VMEM(prompt_weight.shape, BF16),
-            pltpu.VMEM(time_weight.shape, BF16),
-            pltpu.VMEM(qkv_weight.shape, BF16),
-            pltpu.SemaphoreType.DMA((11,)),
+            pltpu.SemaphoreType.DMA((4,)),
         ],
         compiler_params=pltpu.CompilerParams(vmem_limit_bytes=VMEM_LIMIT),
         cost_estimate=pl.CostEstimate(
@@ -259,40 +279,60 @@
         ),
         name="prepare",
     )(
-        feats,
+        step_index,
         in_hbm(back),
         in_hbm(ahead),
         in_hbm(latent_weight),
         in_hbm(prompt_weight),
-        in_hbm(time_weight),
-        in_hbm(qkv_weight),
-    )
+        time_weight,
+        qkv_weight,
+    )
+
+
+def weights_of(delta_ref):
+    branch = lax.axis_index("cfg") % 2
+    delta = delta_ref[0:1, 0:1]
+    mine = jnp.where(branch == 0, 1.0 + GUIDE, -GUIDE) * delta
+    other = jnp.where(branch == 0, -GUIDE, 1.0 + GUIDE) * delta
+    return mine, other
+
+
+def updated_end(refs, half, own, whole_block):
+    delta_ref, vel_ref, partner_ref, latent_ref = refs
+
+    def ends(ref, places):
+        head, tail = places
+        return jnp.where(half == 0, ref[:, head : head + HALO], ref[:, tail : tail + HALO])
+
+    mine, other = weights_of(delta_ref)
+    return (
+        ends(latent_ref, whole_block)
+        + (mine * ends(vel_ref, own) + other * ends(partner_ref, own).astype(F32))
+    ).astype(BF16)
+
+
+def far_kernel(delta_ref, vel_ref, partner_ref, latent_ref, prompt_ref, far_ref):
+    half, _, _ = location()
+    mel, frames = vel_ref.shape
+    last = 2 * frames - HALO
+    far_ref[0:mel] = updated_end(
+        (delta_ref, vel_ref, partner_ref, latent_ref), half, (0, frames - HALO), (0, last)
+    )
+    far_ref[mel : 2 * mel] = jnp.where(
+        half == 0, prompt_ref[:, :HALO], prompt_ref[:, last:]
+    ).astype(BF16)
 
 
 def combine_kernel(
-    delta_ref,
-    vel_ref,
-    partner_ref,
-    latent_ref,
-    prompt_ref,
-    next_ref,
-    rows_ref,
-    seq_ref,
-    cross_ref,
+    delta_ref, vel_ref, partner_ref, latent_ref, prompt_ref, next_ref, rows_ref, cross_ref
 ):
     half, branch, _ = location()
     mel, frames = vel_ref.shape
-    delta = delta_ref[0]
-    mine = jnp.where(branch == 0, 1.0 + GUIDE, -GUIDE) * delta
-    other = jnp.where(branch == 0, -GUIDE, 1.0 + GUIDE) * delta
+    mine, other = weights_of(delta_ref)
     latent = jnp.where(half == 0, latent_ref[:, :frames], latent_ref[:, frames:])
     prompt = jnp.where(half == 0, prompt_ref[:, :frames], prompt_ref[:, frames:])
     updated = latent + (mine * vel_ref[...] + other * partner_ref[...].astype(F32))
     head, tail = updated[:, :HALO], updated[:, frames - HALO :]
-    seq_ref[0:mel] = jnp.where(half == 0, head, tail).astype(BF16)
-    seq_ref[mel : 2 * mel] = jnp.where(
-        half == 0, prompt[:, :HALO], prompt[:, frames - HALO :]
-    ).astype(BF16)
     cross_ref[...] = jnp.where(half == 0, tail, head).astype(BF16)
     share = frames // 2
     next_ref[...] = jnp.where(branch == 0, updated[:, :share], updated[:, share:])
@@ -307,16 +347,29 @@
     mel, frames = vel.shape
     return pl.pallas_call(
         combine_kernel,
-        in_specs=[whole(pltpu.SMEM)] + [whole()] * 4,
-        out_specs=[whole()] * 4,
+        in_specs=[whole()] * 5,
+        out_specs=[whole()] * 3,
         out_shape=[
             jax.ShapeDtypeStruct((mel, frames // 2), F32),
             jax.ShapeDtypeStruct((256, frames), BF16),
-            jax.ShapeDtypeStruct((2 * mel, HALO), BF16),
             jax.ShapeDtypeStruct((mel, HALO), BF16),
         ],
         compiler_params=pltpu.CompilerParams(vmem_limit_bytes=SMALL_VMEM),
+        cost_estimate=pl.CostEstimate(
+            flops=5_000_000_000, bytes_accessed=1_000_000, transcendentals=0
+        ),
         name="combine",
+    )(delta, vel, partner, latent, prompt)
+
+
+def far_call(delta, vel, partner, latent, prompt):
+    return pl.pallas_call(
+        far_kernel,
+        in_specs=[whole()] * 5,
+        out_specs=whole(),
+        out_shape=jax.ShapeDtypeStruct((2 * vel.shape[0], HALO), BF16),
+        compiler_params=pltpu.CompilerParams(vmem_limit_bytes=SMALL_VMEM),
+        name="far",
     )(delta, vel, partner, latent, prompt)
 
 
@@ -412,21 +465,37 @@
     )
 
 
-def inner_kernel(
+def edges_of(frames):
+    own = TILE + HALO
+    return (
+        (0, 0, 0, HALO, 0),
+        (frames // TILE - 1, frames - own, HALO, frames + HALO - own, frames + HALO),
+    )
+
+
+def layer_kernel(
     mel,
     own_ref,
     mixed_ref,
     keyed_ref,
     gram_ref,
     bias_ref,
+    embed_ref,
+    gate_ref,
+    out_w_ref,
     query_ref,
     key_ref,
     value_ref,
+    done_ref,
+    first_ref,
+    sums_ref,
+    totals_ref,
     context_ref,
 ):
     frames, width = query_ref.shape
     pairs = width // 128
-    normed = normalised(own_ref[...], gram_ref, mel)
+    own = own_ref[...]
+    normed = normalised(own, gram_ref, mel)
     turned = normed.T
     for start in range(0, width, 256):
         cols = slice(start, start + 256)
@@ -459,62 +528,6 @@
             total = attend(tile, pair, False)
             least = jnp.minimum(least, total)
             most = jnp.maximum(most, total)
-
-    @pl.when(jnp.logical_not(in_range(least, most)))
-    def _():
-        def one(index, carry):
-            attend(first + index // pairs, index % pairs, True)
-            return carry
-
-        lax.fori_loop(0, (last - first) * pairs, one, 0)
-
-
-def inner_call(mel, own, mixed, keyed, gram, bias):
-    frames = own.shape[1]
-    width = keyed.shape[0]
-    return pl.pallas_call(
-        functools.partial(inner_kernel, mel),
-        in_specs=[whole()] * 5,
-        out_specs=[whole()] * 4,
-        out_shape=[
-            jax.ShapeDtypeStruct((frames, width), BF16),
-            jax.ShapeDtypeStruct((width, frames), BF16),
-            jax.ShapeDtypeStruct((frames, 2 * width), BF16),
-            jax.ShapeDtypeStruct((frames - 2 * HALO, width), BF16),
-        ],
-        compiler_params=pltpu.CompilerParams(vmem_limit_bytes=VMEM_LIMIT),
-        cost_estimate=pl.CostEstimate(
-            flops=3_000_000_000, bytes_accessed=6_000_000, transcendentals=3_000_000
-        ),
-        name="inner",
-    )(own, mixed, keyed, gram, bias)
-
-
-def edges_of(frames):
-    own = TILE + HALO
-    return (
-        (0, 0, 0, HALO, 0),
-        (frames // TILE - 1, frames - own, HALO, frames + HALO - own, frames + HALO),
-    )
-
-
-def outer_kernel(
-    own_ref,
-    query_ref,
-    key_ref,
-    value_ref,
-    bias_ref,
-    context_ref,
-    embed_ref,
-    gate_ref,
-    out_w_ref,
-    done_ref,
-    first_ref,
-    sums_ref,
-    totals_ref,
-):
-    frames, width = query_ref.shape
-    pairs = width // 128
     for edge, (tile, at, _, bias_at, _) in enumerate(edges_of(frames)):
         window = pl.ds(at, TILE + HALO)
         here = slice(edge * TILE, (edge + 1) * TILE)
@@ -529,40 +542,55 @@
             sums = pair_sums(scores, *pair_values(value_ref, pair, window))
             sums_ref[here, cols] = sums[:, :128]
             totals_ref[here, cols] = sums[:, 128:]
-    own_turned = own_ref[...].T
+
+    @pl.when(jnp.logical_not(in_range(least, most)))
+    def _():
+        def one(index, carry):
+            attend(first + index // pairs, index % pairs, True)
+            return carry
+
+        lax.fori_loop(0, (last - first) * pairs, one, 0)
+
+    own_turned = own.T
     for start in range(0, width, 256):
         cols = slice(start, start + 256)
-        first = mm(own_turned, embed_ref[:, cols])
+        start_rows = mm(own_turned, embed_ref[:, cols])
         projected = mm(context_ref[...], out_w_ref[:, cols])
         done_ref[:, cols] = (
-            first[HALO : frames - HALO] + gate_ref[:, cols] * projected
+            start_rows[HALO : frames - HALO] + gate_ref[:, cols] * projected
         ).astype(BF16)
-        first_ref[0:HALO, cols] = first[0:HALO]
-        first_ref[HALO : 2 * HALO, cols] = first[frames - HALO :]
-
-
-def outer_call(own, query, key, value, bias, context, embed, gate, out_w):
-    frames, width = query.shape
+        first_ref[0:HALO, cols] = start_rows[0:HALO]
+        first_ref[HALO : 2 * HALO, cols] = start_rows[frames - HALO :]
+
+
+def layer_call(mel, own, mixed, keyed, gram, bias, embed, gate, out_w):
+    frames = own.shape[1]
+    width = out_w.shape[0]
     return pl.pallas_call(
-        outer_kernel,
-        in_specs=[whole()] * 9,
-        out_specs=[whole()] * 4,
+        functools.partial(layer_kernel, mel),
+        in_specs=[whole()] * 8,
+        out_specs=[whole()] * 7,
         out_shape=[
+            jax.ShapeDtypeStruct((frames, width), BF16),
+            jax.ShapeDtypeStruct((width, frames), BF16),
+            jax.ShapeDtypeStruct((frames, 2 * width), BF16),
             jax.ShapeDtypeStruct((frames - 2 * HALO, width), BF16),
             jax.ShapeDtypeStruct((2 * HALO, width), F32),
             jax.ShapeDtypeStruct((2 * TILE, width), F32),
             jax.ShapeDtypeStruct((2 * TILE, width), F32),
         ],
+        scratch_shapes=[pltpu.VMEM((frames - 2 * HALO, width), BF16)],
         compiler_params=pltpu.CompilerParams(vmem_limit_bytes=VMEM_LIMIT),
         cost_estimate=pl.CostEstimate(
-            flops=3_000_000_000, bytes_accessed=6_000_000, transcendentals=2_000_000
+            flops=5_000_000_000, bytes_accessed=6_000_000, transcendentals=2_000_000
         ),
-        name="outer",
-    )(own, query, key, value, bias, context, embed, gate, out_w)
+        name="layer",
+    )(own, mixed, keyed, gram, bias, embed, gate, out_w)
 
 
 def close_kernel(
-    near_ref,
+    far_ref,
+    cross_ref,
     prompt_ref,
     mixed_ref,
     keyed_ref,
@@ -587,7 +615,7 @@
     half, branch, _ = location()
     frames, width = query_ref.shape
     pairs = width // 128
-    mel = near_ref.shape[0] // 3
+    mel = cross_ref.shape[0]
     inner = pltpu.make_async_copy(done_ref, next_ref.at[pl.ds(HALO, frames - 2 * HALO)], sems.at[0])
     inner.start()
     flag = jnp.where(branch == 0, 1.0, 0.0)
@@ -595,11 +623,9 @@
         half == 0, prompt_ref[:, frames : frames + HALO], prompt_ref[:, frames - HALO : frames]
     )
     blank = jnp.zeros((256 - 2 * mel, HALO), F32)
-    near = near_ref[...].astype(F32)
-    cross_rows = jnp.concatenate([near[0:mel], prompt * flag, blank], axis=0)
-    seq_rows = jnp.concatenate(
-        [near[mel : 2 * mel], near[2 * mel : 3 * mel] * flag, blank], axis=0
-    )
+    far = far_ref[...].astype(F32)
+    cross_rows = jnp.concatenate([cross_ref[...].astype(F32), prompt * flag, blank], axis=0)
+    seq_rows = jnp.concatenate([far[0:mel], far[mel:] * flag, blank], axis=0)
     before = jnp.where(half == 0, seq_rows, cross_rows).astype(BF16)
     after = jnp.where(half == 0, cross_rows, seq_rows).astype(BF16)
     normed = normalised(jnp.concatenate([before, after], axis=1), gram_ref, mel)
@@ -680,12 +706,12 @@
 
 
 def close_call(
-    near, prompt, mixed, keyed, gram, bias, query, key, value, sums, totals, first, gate, out_w, done
+    far, cross, prompt, mixed, keyed, gram, bias, query, key, value, sums, totals, first, gate, out_w, done
 ):
     frames, width = query.shape
     return pl.pallas_call(
         close_kernel,
-        in_specs=[whole()] * 15,
+        in_specs=[whole()] * 16,
         out_specs=whole(pltpu.HBM),
         out_shape=jax.ShapeDtypeStruct((frames, width), BF16),
         scratch_shapes=[
@@ -700,7 +726,24 @@
             flops=2_000_000_000, bytes_accessed=6_000_000, transcendentals=1_000_000
         ),
         name="close",
-    )(near, prompt, mixed, keyed, gram, bias, query, key, value, sums, totals, first, gate, out_w, done)
+    )(
+        far,
+        cross,
+        prompt,
+        mixed,
+        keyed,
+        gram,
+        bias,
+        query,
+        key,
+        value,
+        sums,
+        totals,
+        first,
+        gate,
+        out_w,
+        done,
+    )
 
 
 def body(
@@ -719,7 +762,6 @@
 ):
     axes = ("seq", "cfg")
     spans = lax.axis_size("seq")
-    mel = latent.shape[0]
     total_blocks = 2 * spans * (hidden.shape[0] // BLK)
 
     def at(span, cell):
@@ -729,37 +771,33 @@
     to_partner = [(at(s, c), at(s, c ^ 1)) for s, c in everyone]
     to_half = [(at(s, c), at(s, c ^ 3)) for s, c in everyone]
     to_span = [
-        (at(s, c), at(s + (1 if c >= 2 else -1), c))
+        (at(s, c), at(s + (1 if c >= 2 else -1), c ^ 3))
         for s, c in everyone
         if 0 <= s + (1 if c >= 2 else -1) < spans
     ]
     vel, sent = velocity_call(hidden, proj_weight.T)
     sent, step_index = lax.optimization_barrier((sent, step_index))
     partner = lax.ppermute(sent, axes, to_partner)
-    delta = time_value(step_index + 1) - time_value(step_index)
-    feats = time_features(step_index, time_weight.shape[0])
-    mixed, keyed, gram, embed, gate, bias = prepare_call(
+    mixed, keyed, gram, embed, gate, bias, delta = prepare_call(
         total_blocks,
+        step_index,
         window_back,
         window_ahead,
-        feats,
         latent_weight,
         prompt_weight,
         time_weight,
         qkv_weight,
     )
-    partner, gate = lax.optimization_barrier((partner, gate))
-    latent_out, own, far, cross = combine_call(delta, vel, partner, latent, prompt_mel)
-    relayed = lax.ppermute(far, axes, to_span)
-    query, key, value, context = inner_call(mel, own, mixed, keyed, gram, bias)
-    near = jnp.concatenate([cross, relayed], axis=0)
-    near, context = lax.optimization_barrier((near, context))
-    near = lax.ppermute(near, axes, to_half)
-    done, first, sums, totals = outer_call(
-        own, query, key, value, bias, context, embed, gate, attn_out_weight
+    far = far_call(delta, vel, partner, latent, prompt_mel)
+    far = lax.ppermute(far, axes, to_span)
+    latent_out, own, cross = combine_call(delta, vel, partner, latent, prompt_mel)
+    cross = lax.ppermute(cross, axes, to_half)
+    query, key, value, done, first, sums, totals = layer_call(
+        latent.shape[0], own, mixed, keyed, gram, bias, embed, gate, attn_out_weight
     )
     hidden_next = close_call(
-        near,
+        far,
+        cross,
         prompt_mel,
         mixed,
         keyed,

time: 48.8 us -> 46.1 us (0.945)
  waiting for transfers between devices: 3.43 us -> 0.37 us
  starting transfers between devices: 9.84 us -> 12.5 us
  Pallas kernels: 33.8 us -> 31.7 us
    ppermute x2, waiting for transfers between devices: 3.43 us -> 0.01 us  [the longest x1 0.01 us: body(): far = lax.ppermute(far, axes, to_span)]
    ppermute x2, starting transfers between devices: 6.48 us -> 9.14 us  [the longest x1 9.14 us: body(): far = lax.ppermute(far, axes, to_span)]
    pallas_call x1, Pallas kernels: 4.63 us -> 3.12 us  [prepare_call(): pl.pallas_call(functools.partial(prepare_kernel, total_blocks), in_specs=...]
    pallas_call x1, Pallas kernels: 3 us -> 2.32 us  [velocity_call(): pl.pallas_call(velocity_kernel, in_specs=[whole(pltpu.HBM)] * 2, out_spec...]
  transfers between devices with their start and end apart: 3 -> 3, of which waited for: 1 -> 1; matrix products, arithmetic and copies ran while one was open for 0% -> 0% of each run, Pallas kernels for 37% -> 38%
where the time goes in v3:
time: 46.1 us; the launch traced here: 46 us
  Pallas kernels  31.7 us (69%)
  starting transfers between devices  12.5 us (27%)
  between operations  1.41 us (3%)
    pallas_call x1, Pallas kernels, layer_call(): pl.pallas_call(functools.partial(layer_kernel, mel), in_specs=[whole()] *...  13.5 us
    pallas_call x1, Pallas kernels, close_call(): pl.pallas_call(close_kernel, in_specs=[whole()] * 16, out_specs=whole(plt...  11.9 us
    ppermute x1, starting transfers between devices, body(): far = lax.ppermute(far, axes, to_span)  9.14 us
    ppermute x1, starting transfers between devices, body(): partner = lax.ppermute(sent, axes, to_partner)  3.36 us
    pallas_call x1, Pallas kernels, prepare_call(): pl.pallas_call(functools.partial(prepare_kernel, total_blocks), in_specs=...  3.12 us
    pallas_call x1, Pallas kernels, velocity_call(): pl.pallas_call(velocity_kernel, in_specs=[whole(pltpu.HBM)] * 2, out_spec...  2.32 us
  transfers between devices with their start and end apart: 3, of which 1 were waited for; matrix products, arithmetic and copies ran while one was open for 0% of the time, Pallas kernels for 38%

profile of v3, /device:TPU:6, one launch (start us, length us, event | category | flops | bytes accessed | tf_op | source)
XLA Modules:
  0.0 46.0 jit_solution(9354450706556277607)
XLA Ops:
  0.6 0.0 slice-start
  0.6 0.0 slice-start.1
  0.7 0.0 copy-start.1
  0.7 2.3 %velocity.1 = (f32[80,512]{1,0:T(8,128)S(1)}, bf16[80,512]{1,0:T(8,128)(2,1)S(1)}) custom-call(bf16[512,1024]{1,0:T(8,128)(2,1)} %hidden_ref.1, bf16[80,1024]{1,0:T(8,128)(2,1)} %bitcast.3), custom_call_target="tpu_custom_call" | custom-call | flops 10000000000 | bytes 1048576 | tf_op jit(solution)/shard_map/velocity/pallas_call | solution.py:119
  3.0 3.4 %collective-permute-start = (bf16[80,512]{1,0:T(8,128)(2,1)S(1)}, bf16[80,512]{1,0:T(8,128)(2,1)S(1)}, u32[]{:S(2)}, u32[]{:S(2)}) collective-permute-start(bf16[80,512]{1,0:T(8,128)(2,1)S(1)} %get-tuple-element.27), channel_id=1, source_target_pairs={{0,1},{1,0},{2,3},{3,2},{4,5},{5,4},{6,7},{7,6},{8,9},{9,8},{10,11... | collective-permute-start | bytes 245768 | tf_op jit(solution)/shard_map/ppermute | solution.py:780
  7.0 0.0 slice-done
  7.0 0.0 slice-done.1
  7.0 0.0 copy-done.1
  7.0 0.0 copy-start.2
  7.1 0.0 copy-start.3
  7.1 3.1 %prepare.1 = (bf16[256,2048]{1,0:T(8,128)(2,1)S(1)}, bf16[1024,256]{1,0:T(8,128)(2,1)S(1)}, bf16[512,256]{1,0:T(8,128)(2,1)S(1)}, bf16[256,1024]{1,0:T(8,128)(2,...) custom-call(s32[1]{0:T(128)S(6)} %copy.14.step_ref, s32[32]{0:T(128)} %back_hbm.1, ...), custom_call_target="tpu_custom_call" | custom-call | flops 1610612736 | bytes 8388608 | tf_op jit(solution)/shard_map/prepare/pallas_call | solution.py:255
  10.2 0.4 collective-permute-done.partner_ref
  10.6 0.0 copy-done.2
  10.6 0.0 copy-done.3
  10.6 0.1 far.1
  10.7 0.0 copy-start
  10.7 9.1 %collective-permute-start.1 = (bf16[160,128]{1,0:T(8,128)(2,1)S(1)}, bf16[160,128]{1,0:T(8,128)(2,1)S(1)}, u32[]{:S(2)}, u32[]{:S(2)}) collective-permute-start(bf16[160,128]{1,0:T(8,128)(2,1)S(1)} %far.1), channel_id=1, source_target_pairs={{2,5},{3,4},{4,3},{5,2},{6,9},{7,8},{8,7},{9,6},{10,13},{11,12},{1... | collective-permute-start | bytes 122888 | tf_op jit(solution)/shard_map/ppermute | solution.py:792
  19.8 0.8 %combine.1 = (f32[80,256]{1,0:T(8,128)}, bf16[256,512]{1,0:T(8,128)(2,1)S(1)}, bf16[80,128]{1,0:T(8,128)(2,1)S(1)}) custom-call(f32[1,128]{1,0:T(1,128)S(1)} %get-tuple-element.25.delta_ref, f32[80,512]{1,0:T(8,128)S(1)} %get-tuple-element.26.vel_ref, bf16[80,512]{1,0:T(8,128)(2,1)S(1)} %collective-permute-done.partner_ref, f32[80,1024]{1,0:T(8,128)S(1)} %copy-done.3, ...), custom_call_target="tpu_custom_call" | custom-call | flops 5000000000 | bytes 1000000 | tf_op jit(solution)/shard_map/combine/pallas_call | solution.py:348
  20.6 0.0 collective-permute-start.2
  20.6 0.0 copy-done
  20.6 13.5 %layer.1 = (bf16[512,1024]{1,0:T(8,128)(2,1)S(1)}, bf16[1024,512]{1,0:T(8,128)(2,1)S(1)}, bf16[512,2048]{1,0:T(8,128)(2,1)S(1)}, bf16[256,1024]{1,0:T(8,128)(2,1...) custom-call(bf16[256,512]{1,0:T(8,128)(2,1)S(1)} %get-tuple-element.34.own_ref, ...), custom_call_target="tpu_custom_call" | custom-call | flops 5000000000 | bytes 6000000 | tf_op jit(solution)/shard_map/layer/pallas_call | solution.py:569
  34.1 0.0 collective-permute-done.2.cross_ref
  34.1 0.0 collective-permute-done.1.far_ref
  34.1 11.9 %close.1 = bf16[512,1024]{1,0:T(8,128)(2,1)} custom-call(bf16[160,128]{1,0:T(8,128)(2,1)S(1)} %collective-permute-done.1.far_ref, bf16[80,128]{1,0:T(8,128)(2,1)S(1)} %collective-permute-done.2.cross_ref, f32[80,1024]{1,0:T(8,128)S(1)} %copy-done.2, bf16[256,2048]{1,0:T(8,128)(2,1)S(1)} %get-tuple-element.30.mixed_ref, ...), custom_call_target="tpu_custom_call" | custom-call | flops 2000000000 | bytes 6000000 | tf_op jit(solution)/shard_map/close/pallas_call | solution.py:712
  (1 shorter events, 0.0 us)
Async XLA Ops:
  0.6 6.4 %slice-start = ((s8[6291456]{0:T(1024)(128)(4,1)}), s8[4194304]{0:T(1024)(128)(4,1)S(1)}, s32[]{:S(2)}) async-start(s8[6291456]{0:T(1024)(128)(4,1)} %bitcast.1), calls=%async_computation | async-start | bytes 8388608
  0.6 6.4 %slice-start.1 = ((s8[6291456]{0:T(1024)(128)(4,1)}), s8[2097152]{0:T(1024)(128)(4,1)S(1)}, s32[]{:S(2)}) async-start(s8[6291456]{0:T(1024)(128)(4,1)} %bitcast.1), calls=%async_computation.1 | async-start | bytes 4194304
  0.7 6.4 %copy-start.1 = (bf16[256,3072]{1,0:T(8,128)(2,1)S(1)}, bf16[256,3072]{1,0:T(8,128)(2,1)}, u32[]{:S(2)}) copy-start(bf16[256,3072]{1,0:T(8,128)(2,1)} %time_w_ref.1) | copy-start | bytes 4718596
  3.0 7.6 %collective-permute-start = (bf16[80,512]{1,0:T(8,128)(2,1)S(1)}, bf16[80,512]{1,0:T(8,128)(2,1)S(1)}, u32[]{:S(2)}, u32[]{:S(2)}) collective-permute-start(bf16[80,512]{1,0:T(8,128)(2,1)S(1)} %get-tuple-element.27), channel_id=1, source_target_pairs={{0,1},{1,0},{2,3},{3,2},{4,5},{5,4},{6,7},{7,6},{8,9},{9,8},{10,11... | collective-permute-start | bytes 245768 | tf_op jit(solution)/shard_map/ppermute | solution.py:780
  7.0 3.5 %copy-start.2 = (f32[80,1024]{1,0:T(8,128)S(1)}, f32[80,1024]{1,0:T(8,128)}, u32[]{:S(2)}) copy-start(f32[80,1024]{1,0:T(8,128)} %prompt_ref.5) | copy-start | bytes 983044
  7.1 3.5 %copy-start.3 = (f32[80,1024]{1,0:T(8,128)S(1)}, f32[80,1024]{1,0:T(8,128)}, u32[]{:S(2)}) copy-start(f32[80,1024]{1,0:T(8,128)} %latent_ref.3) | copy-start | bytes 983044
  10.7 9.9 %copy-start = (bf16[1024,1024]{1,0:T(8,128)(2,1)S(1)}, bf16[1024,1024]{1,0:T(8,128)(2,1)}, u32[]{:S(2)}) copy-start(bf16[1024,1024]{1,0:T(8,128)(2,1)} %out_w_ref.3) | copy-start | bytes 6291460
  10.7 23.4 %collective-permute-start.1 = (bf16[160,128]{1,0:T(8,128)(2,1)S(1)}, bf16[160,128]{1,0:T(8,128)(2,1)S(1)}, u32[]{:S(2)}, u32[]{:S(2)}) collective-permute-start(bf16[160,128]{1,0:T(8,128)(2,1)S(1)} %far.1), channel_id=1, source_target_pairs={{2,5},{3,4},{4,3},{5,2},{6,9},{7,8},{8,7},{9,6},{10,13},{11,12},{1... | collective-permute-start | bytes 122888 | tf_op jit(solution)/shard_map/ppermute | solution.py:792
  20.6 13.5 %collective-permute-start.2 = (bf16[80,128]{1,0:T(8,128)(2,1)S(1)}, bf16[80,128]{1,0:T(8,128)(2,1)S(1)}, u32[]{:S(2)}, u32[]{:S(2)}) collective-permute-start(bf16[80,128]{1,0:T(8,128)(2,1)S(1)} %get-tuple-element.29), channel_id=1, source_target_pairs={{0,3},{1,2},{2,1},{3,0},{4,7},{5,6},{6,5},{7,4},{8,11},{9,10},{10,... | collective-permute-start | bytes 61448 | tf_op jit(solution)/shard_map/ppermute | solution.py:794

commit v4 on v3

--- a/solution.py
+++ b/solution.py
@@ -475,6 +475,7 @@
 
 def layer_kernel(
     mel,
+    share_ref,
     own_ref,
     mixed_ref,
     keyed_ref,
@@ -483,6 +484,7 @@
     embed_ref,
     gate_ref,
     out_w_ref,
+    latent_ref,
     query_ref,
     key_ref,
     value_ref,
@@ -491,7 +493,10 @@
     sums_ref,
     totals_ref,
     context_ref,
+    sems,
 ):
+    share = pltpu.make_async_copy(share_ref, latent_ref, sems.at[0])
+    share.start()
     frames, width = query_ref.shape
     pairs = width // 128
     own = own_ref[...]
@@ -543,6 +548,20 @@
             sums_ref[here, cols] = sums[:, :128]
             totals_ref[here, cols] = sums[:, 128:]
 
+    def project():
+        own_turned = own_ref[...].T
+        for start in range(0, width, 512):
+            cols = slice(start, start + 512)
+            start_rows = mm(own_turned, embed_ref[:, cols])
+            projected = mm(context_ref[...], out_w_ref[:, cols])
+            done_ref[:, cols] = (
+                start_rows[HALO : frames - HALO] + gate_ref[:, cols] * projected
+            ).astype(BF16)
+            first_ref[0:HALO, cols] = start_rows[0:HALO]
+            first_ref[HALO : 2 * HALO, cols] = start_rows[frames - HALO :]
+
+    project()
+
     @pl.when(jnp.logical_not(in_range(least, most)))
     def _():
         def one(index, carry):
@@ -550,27 +569,20 @@
             return carry
 
         lax.fori_loop(0, (last - first) * pairs, one, 0)
-
-    own_turned = own.T
-    for start in range(0, width, 256):
-        cols = slice(start, start + 256)
-        start_rows = mm(own_turned, embed_ref[:, cols])
-        projected = mm(context_ref[...], out_w_ref[:, cols])
-        done_ref[:, cols] = (
-            start_rows[HALO : frames - HALO] + gate_ref[:, cols] * projected
-        ).astype(BF16)
-        first_ref[0:HALO, cols] = start_rows[0:HALO]
-        first_ref[HALO : 2 * HALO, cols] = start_rows[frames - HALO :]
-
-
-def layer_call(mel, own, mixed, keyed, gram, bias, embed, gate, out_w):
-    frames = own.shape[1]
+        project()
+
+    share.wait()
+
+
+def layer_call(share, own, mixed, keyed, gram, bias, embed, gate, out_w):
+    mel, frames = share.shape[0], own.shape[1]
     width = out_w.shape[0]
     return pl.pallas_call(
         functools.partial(layer_kernel, mel),
-        in_specs=[whole()] * 8,
-        out_specs=[whole()] * 7,
+        in_specs=[whole()] * 9,
+        out_specs=[whole(pltpu.HBM)] + [whole()] * 7,
         out_shape=[
+            jax.ShapeDtypeStruct(share.shape, F32),
             jax.ShapeDtypeStruct((frames, width), BF16),
             jax.ShapeDtypeStruct((width, frames), BF16),
             jax.ShapeDtypeStruct((frames, 2 * width), BF16),
@@ -579,13 +591,16 @@
             jax.ShapeDtypeStruct((2 * TILE, width), F32),
             jax.ShapeDtypeStruct((2 * TILE, width), F32),
         ],
-        scratch_shapes=[pltpu.VMEM((frames - 2 * HALO, width), BF16)],
+        scratch_shapes=[
+            pltpu.VMEM((frames - 2 * HALO, width), BF16),
+            pltpu.SemaphoreType.DMA((1,)),
+        ],
         compiler_params=pltpu.CompilerParams(vmem_limit_bytes=VMEM_LIMIT),
         cost_estimate=pl.CostEstimate(
             flops=5_000_000_000, bytes_accessed=6_000_000, transcendentals=2_000_000
         ),
         name="layer",
-    )(own, mixed, keyed, gram, bias, embed, gate, out_w)
+    )(share, own, mixed, keyed, gram, bias, embed, gate, out_w)
 
 
 def close_kernel(
@@ -657,8 +672,36 @@
             least = jnp.minimum(least, total)
             most = jnp.maximum(most, total)
 
+    columns = 256
+    copies = []
+    for start in range(0, width, columns):
+        for edge, row in enumerate((0, frames - HALO)):
+            cols = pl.ds(start, columns)
+            copies.append(
+                pltpu.make_async_copy(
+                    edge_ref.at[pl.ds(edge * HALO, HALO), cols],
+                    next_ref.at[pl.ds(row, HALO), cols],
+                    sems.at[1 + len(copies)],
+                )
+            )
+
+    def finish():
+        for index, start in enumerate(range(0, width, columns)):
+            cols = slice(start, start + columns)
+            projected = mm(context_ref[...], out_w_ref[:, cols])
+            edge_ref[:, cols] = (first_ref[:, cols] + gate_ref[:, cols] * projected).astype(BF16)
+            copies[2 * index].start()
+            copies[2 * index + 1].start()
+
+    def settle():
+        for copy in copies:
+            copy.wait()
+
+    finish()
+
     @pl.when(jnp.logical_not(in_range(least, most)))
     def _():
+        settle()
         for edge, (tile, at, near_at, bias_own, bias_near) in enumerate(edges):
             here = slice(edge * TILE, (edge + 1) * TILE)
 
@@ -690,19 +733,10 @@
 
             lax.fori_loop(0, pairs, one, 0)
 
-    for start in range(0, width, 256):
-        cols = slice(start, start + 256)
-        projected = mm(context_ref[...], out_w_ref[:, cols])
-        edge_ref[:, cols] = (first_ref[:, cols] + gate_ref[:, cols] * projected).astype(BF16)
-    head = pltpu.make_async_copy(edge_ref.at[pl.ds(0, HALO)], next_ref.at[pl.ds(0, HALO)], sems.at[1])
-    tail = pltpu.make_async_copy(
-        edge_ref.at[pl.ds(HALO, HALO)], next_ref.at[pl.ds(frames - HALO, HALO)], sems.at[2]
-    )
-    head.start()
-    tail.start()
+        finish()
+
     inner.wait()
-    head.wait()
-    tail.wait()
+    settle()
 
 
 def close_call(
@@ -719,7 +753,7 @@
             pltpu.VMEM((2 * HALO, 2 * width), BF16),
             pltpu.VMEM((2 * TILE, width), BF16),
             pltpu.VMEM((2 * TILE, width), BF16),
-            pltpu.SemaphoreType.DMA((3,)),
+            pltpu.SemaphoreType.DMA((9,)),
         ],
         compiler_params=pltpu.CompilerParams(vmem_limit_bytes=VMEM_LIMIT),
         cost_estimate=pl.CostEstimate(
@@ -790,10 +824,10 @@
     )
     far = far_call(delta, vel, partner, latent, prompt_mel)
     far = lax.ppermute(far, axes, to_span)
-    latent_out, own, cross = combine_call(delta, vel, partner, latent, prompt_mel)
+    share, own, cross = combine_call(delta, vel, partner, latent, prompt_mel)
     cross = lax.ppermute(cross, axes, to_half)
-    query, key, value, done, first, sums, totals = layer_call(
-        latent.shape[0], own, mixed, keyed, gram, bias, embed, gate, attn_out_weight
+    latent_out, query, key, value, done, first, sums, totals = layer_call(
+        share, own, mixed, keyed, gram, bias, embed, gate, attn_out_weight
     )
     hidden_next = close_call(
         far,

time: 46.1 us -> 47.6 us (1.033)
  Pallas kernels: 31.7 us -> 33 us
    pallas_call x1, Pallas kernels: 11.9 us -> 13 us  [close_call(): pl.pallas_call(close_kernel, in_specs=[whole()] * 16, out_specs=whole(plt...]
    pallas_call x1, Pallas kernels: 13.5 us -> 14.3 us  [layer_call(): pl.pallas_call(functools.partial(layer_kernel, mel), in_specs=[whole()] *...]
    pallas_call x1, Pallas kernels: 0.77 us -> 0.15 us  [combine_call(): pl.pallas_call(combine_kernel, in_specs=[whole()] * 5, out_specs=[whole()...]
  transfers between devices with their start and end apart: 3 -> 3, of which waited for: 1 -> 1; matrix products, arithmetic and copies ran while one was open for 0% -> 0% of each run, Pallas kernels for 38% -> 37%
where the time goes in v4:
time: 47.6 us; the launch traced here: 47.5 us
  Pallas kernels  33 us (69%)
  starting transfers between devices  12.6 us (26%)
  between operations  1.43 us (3%)
    pallas_call x1, Pallas kernels, layer_call(): pl.pallas_call(functools.partial(layer_kernel, mel), in_specs=[whole()] *...  14.3 us
    pallas_call x1, Pallas kernels, close_call(): pl.pallas_call(close_kernel, in_specs=[whole()] * 16, out_specs=whole(plt...  13 us
    ppermute x1, starting transfers between devices, body(): far = lax.ppermute(far, axes, to_span)  9.14 us
    ppermute x1, starting transfers between devices, body(): partner = lax.ppermute(sent, axes, to_partner)  3.36 us
    pallas_call x1, Pallas kernels, prepare_call(): pl.pallas_call(functools.partial(prepare_kernel, total_blocks), in_specs=...  3.11 us
    pallas_call x1, Pallas kernels, velocity_call(): pl.pallas_call(velocity_kernel, in_specs=[whole(pltpu.HBM)] * 2, out_spec...  2.32 us
  transfers between devices with their start and end apart: 3, of which 1 were waited for; matrix products, arithmetic and copies ran while one was open for 0% of the time, Pallas kernels for 37%

profile of v4, /device:TPU:6, one launch (start us, length us, event | category | flops | bytes accessed | tf_op | source)
XLA Modules:
  0.0 47.5 jit_solution(14414921430168181112)
XLA Ops:
  0.6 0.0 slice-start
  0.6 0.0 slice-start.1
  0.7 0.0 copy-start.1
  0.7 2.3 %velocity.1 = (f32[80,512]{1,0:T(8,128)S(1)}, bf16[80,512]{1,0:T(8,128)(2,1)S(1)}) custom-call(bf16[512,1024]{1,0:T(8,128)(2,1)} %hidden_ref.1, bf16[80,1024]{1,0:T(8,128)(2,1)} %bitcast.3), custom_call_target="tpu_custom_call" | custom-call | flops 10000000000 | bytes 1048576 | tf_op jit(solution)/shard_map/velocity/pallas_call | solution.py:119
  3.0 3.4 %collective-permute-start = (bf16[80,512]{1,0:T(8,128)(2,1)S(1)}, bf16[80,512]{1,0:T(8,128)(2,1)S(1)}, u32[]{:S(2)}, u32[]{:S(2)}) collective-permute-start(bf16[80,512]{1,0:T(8,128)(2,1)S(1)} %get-tuple-element.28), channel_id=1, source_target_pairs={{0,1},{1,0},{2,3},{3,2},{4,5},{5,4},{6,7},{7,6},{8,9},{9,8},{10,11... | collective-permute-start | bytes 245768 | tf_op jit(solution)/shard_map/ppermute | solution.py:814
  7.0 0.0 slice-done
  7.0 0.0 slice-done.1
  7.0 0.0 copy-done.1
  7.0 0.0 copy-start.2
  7.1 0.0 copy-start.3
  7.1 3.1 %prepare.1 = (bf16[256,2048]{1,0:T(8,128)(2,1)S(1)}, bf16[1024,256]{1,0:T(8,128)(2,1)S(1)}, bf16[512,256]{1,0:T(8,128)(2,1)S(1)}, bf16[256,1024]{1,0:T(8,128)(2,...) custom-call(s32[1]{0:T(128)S(6)} %copy.14.step_ref, s32[32]{0:T(128)} %back_hbm.1, ...), custom_call_target="tpu_custom_call" | custom-call | flops 1610612736 | bytes 8388608 | tf_op jit(solution)/shard_map/prepare/pallas_call | solution.py:255
  10.2 0.4 collective-permute-done.partner_ref
  10.6 0.0 copy-done.2
  10.6 0.0 copy-done.3
  10.6 0.1 far.1
  10.7 0.0 copy-start
  10.7 9.1 %collective-permute-start.1 = (bf16[160,128]{1,0:T(8,128)(2,1)S(1)}, bf16[160,128]{1,0:T(8,128)(2,1)S(1)}, u32[]{:S(2)}, u32[]{:S(2)}) collective-permute-start(bf16[160,128]{1,0:T(8,128)(2,1)S(1)} %far.1), channel_id=1, source_target_pairs={{2,5},{3,4},{4,3},{5,2},{6,9},{7,8},{8,7},{9,6},{10,13},{11,12},{1... | collective-permute-start | bytes 122888 | tf_op jit(solution)/shard_map/ppermute | solution.py:826
  19.8 0.2 combine.1
  20.0 0.1 collective-permute-start.2
  20.1 0.0 copy-done
  20.1 14.3 %layer.1 = (f32[80,256]{1,0:T(8,128)}, bf16[512,1024]{1,0:T(8,128)(2,1)S(1)}, bf16[1024,512]{1,0:T(8,128)(2,1)S(1)}, bf16[512,2048]{1,0:T(8,128)(2,1)S(1)}, bf16...) custom-call(f32[80,256]{1,0:T(8,128)S(1)} %get-tuple-element.29.share_re, ...), custom_call_target="tpu_custom_call" | custom-call | flops 5000000000 | bytes 6000000 | tf_op jit(solution)/shard_map/layer/pallas_call | solution.py:580
  34.4 0.0 collective-permute-done.2.cross_ref
  34.4 0.0 collective-permute-done.1.far_ref
  34.4 13.0 %close.1 = bf16[512,1024]{1,0:T(8,128)(2,1)} custom-call(bf16[160,128]{1,0:T(8,128)(2,1)S(1)} %collective-permute-done.1.far_ref, bf16[80,128]{1,0:T(8,128)(2,1)S(1)} %collective-permute-done.2.cross_ref, f32[80,1024]{1,0:T(8,128)S(1)} %copy-done.2, bf16[256,2048]{1,0:T(8,128)(2,1)S(1)} %get-tuple-element.31.mixed_ref, ...), custom_call_target="tpu_custom_call" | custom-call | flops 2000000000 | bytes 6000000 | tf_op jit(solution)/shard_map/close/pallas_call | solution.py:746
  (1 shorter events, 0.0 us)
Async XLA Ops:
  0.6 6.4 %slice-start = ((s8[6291456]{0:T(1024)(128)(4,1)}), s8[4194304]{0:T(1024)(128)(4,1)S(1)}, s32[]{:S(2)}) async-start(s8[6291456]{0:T(1024)(128)(4,1)} %bitcast.1), calls=%async_computation | async-start | bytes 8388608
  0.6 6.4 %slice-start.1 = ((s8[6291456]{0:T(1024)(128)(4,1)}), s8[2097152]{0:T(1024)(128)(4,1)S(1)}, s32[]{:S(2)}) async-start(s8[6291456]{0:T(1024)(128)(4,1)} %bitcast.1), calls=%async_computation.1 | async-start | bytes 4194304
  0.7 6.4 %copy-start.1 = (bf16[256,3072]{1,0:T(8,128)(2,1)S(1)}, bf16[256,3072]{1,0:T(8,128)(2,1)}, u32[]{:S(2)}) copy-start(bf16[256,3072]{1,0:T(8,128)(2,1)} %time_w_ref.1) | copy-start | bytes 4718596
  3.0 7.6 %collective-permute-start = (bf16[80,512]{1,0:T(8,128)(2,1)S(1)}, bf16[80,512]{1,0:T(8,128)(2,1)S(1)}, u32[]{:S(2)}, u32[]{:S(2)}) collective-permute-start(bf16[80,512]{1,0:T(8,128)(2,1)S(1)} %get-tuple-element.28), channel_id=1, source_target_pairs={{0,1},{1,0},{2,3},{3,2},{4,5},{5,4},{6,7},{7,6},{8,9},{9,8},{10,11... | collective-permute-start | bytes 245768 | tf_op jit(solution)/shard_map/ppermute | solution.py:814
  7.0 3.5 %copy-start.2 = (f32[80,1024]{1,0:T(8,128)S(1)}, f32[80,1024]{1,0:T(8,128)}, u32[]{:S(2)}) copy-start(f32[80,1024]{1,0:T(8,128)} %prompt_ref.5) | copy-start | bytes 983044
  7.1 3.5 %copy-start.3 = (f32[80,1024]{1,0:T(8,128)S(1)}, f32[80,1024]{1,0:T(8,128)}, u32[]{:S(2)}) copy-start(f32[80,1024]{1,0:T(8,128)} %latent_ref.3) | copy-start | bytes 983044
  10.7 9.4 %copy-start = (bf16[1024,1024]{1,0:T(8,128)(2,1)S(1)}, bf16[1024,1024]{1,0:T(8,128)(2,1)}, u32[]{:S(2)}) copy-start(bf16[1024,1024]{1,0:T(8,128)(2,1)} %out_w_ref.3) | copy-start | bytes 6291460
  10.7 23.8 %collective-permute-start.1 = (bf16[160,128]{1,0:T(8,128)(2,1)S(1)}, bf16[160,128]{1,0:T(8,128)(2,1)S(1)}, u32[]{:S(2)}, u32[]{:S(2)}) collective-permute-start(bf16[160,128]{1,0:T(8,128)(2,1)S(1)} %far.1), channel_id=1, source_target_pairs={{2,5},{3,4},{4,3},{5,2},{6,9},{7,8},{8,7},{9,6},{10,13},{11,12},{1... | collective-permute-start | bytes 122888 | tf_op jit(solution)/shard_map/ppermute | solution.py:826
  20.0 14.4 %collective-permute-start.2 = (bf16[80,128]{1,0:T(8,128)(2,1)S(1)}, bf16[80,128]{1,0:T(8,128)(2,1)S(1)}, u32[]{:S(2)}, u32[]{:S(2)}) collective-permute-start(bf16[80,128]{1,0:T(8,128)(2,1)S(1)} %get-tuple-element.38), channel_id=1, source_target_pairs={{0,3},{1,2},{2,1},{3,0},{4,7},{5,6},{6,5},{7,4},{8,11},{9,10},{10,... | collective-permute-start | bytes 61448 | tf_op jit(solution)/shard_map/ppermute | solution.py:828

commit v5 on v4

--- a/solution.py
+++ b/solution.py
@@ -655,11 +655,11 @@
     edges = edges_of(frames)
     least = jnp.full((TILE, 128), 1.0, F32)
     most = jnp.full((TILE, 128), 1.0, F32)
-    for edge, (tile, _, near_at, _, bias_at) in enumerate(edges):
-        window = pl.ds(near_at, HALO)
-        here = slice(edge * TILE, (edge + 1) * TILE)
-        for pair in range(pairs):
-            cols = slice(pair * 128, (pair + 1) * 128)
+    for pair in range(pairs):
+        cols = slice(pair * 128, (pair + 1) * 128)
+        for edge, (tile, _, near_at, _, bias_at) in enumerate(edges):
+            window = pl.ds(near_at, HALO)
+            here = slice(edge * TILE, (edge + 1) * TILE)
             queries = pair_queries(query_ref[tile * TILE : (tile + 1) * TILE, cols], tile)
             scores = pair_scores(
                 queries,

time: 47.6 us -> 47.6 us (level)
  no operation moved by 1% of the time
where the time goes in v5:
time: 47.6 us; the launch traced here: 47.4 us
  Pallas kernels  33 us (69%)
  starting transfers between devices  12.6 us (26%)
  between operations  1.43 us (3%)
    pallas_call x1, Pallas kernels, layer_call(): pl.pallas_call(functools.partial(layer_kernel, mel), in_specs=[whole()] *...  14.3 us
    pallas_call x1, Pallas kernels, close_call(): pl.pallas_call(close_kernel, in_specs=[whole()] * 16, out_specs=whole(plt...  13 us
    ppermute x1, starting transfers between devices, body(): far = lax.ppermute(far, axes, to_span)  9.14 us
    ppermute x1, starting transfers between devices, body(): partner = lax.ppermute(sent, axes, to_partner)  3.36 us
    pallas_call x1, Pallas kernels, prepare_call(): pl.pallas_call(functools.partial(prepare_kernel, total_blocks), in_specs=...  3.11 us
    pallas_call x1, Pallas kernels, velocity_call(): pl.pallas_call(velocity_kernel, in_specs=[whole(pltpu.HBM)] * 2, out_spec...  2.32 us
  transfers between devices with their start and end apart: 3, of which 1 were waited for; matrix products, arithmetic and copies ran while one was open for 0% of the time, Pallas kernels for 37%

profile of v5, /device:TPU:6, one launch (start us, length us, event | category | flops | bytes accessed | tf_op | source)
XLA Modules:
  0.0 47.4 jit_solution(4003200592581188170)
XLA Ops:
  0.6 0.0 slice-start
  0.6 0.0 slice-start.1
  0.7 0.0 copy-start.1
  0.7 2.3 %velocity.1 = (f32[80,512]{1,0:T(8,128)S(1)}, bf16[80,512]{1,0:T(8,128)(2,1)S(1)}) custom-call(bf16[512,1024]{1,0:T(8,128)(2,1)} %hidden_ref.1, bf16[80,1024]{1,0:T(8,128)(2,1)} %bitcast.3), custom_call_target="tpu_custom_call" | custom-call | flops 10000000000 | bytes 1048576 | tf_op jit(solution)/shard_map/velocity/pallas_call | solution.py:119
  3.0 3.4 %collective-permute-start = (bf16[80,512]{1,0:T(8,128)(2,1)S(1)}, bf16[80,512]{1,0:T(8,128)(2,1)S(1)}, u32[]{:S(2)}, u32[]{:S(2)}) collective-permute-start(bf16[80,512]{1,0:T(8,128)(2,1)S(1)} %get-tuple-element.28), channel_id=1, source_target_pairs={{0,1},{1,0},{2,3},{3,2},{4,5},{5,4},{6,7},{7,6},{8,9},{9,8},{10,11... | collective-permute-start | bytes 245768 | tf_op jit(solution)/shard_map/ppermute | solution.py:814
  7.0 0.0 slice-done
  7.0 0.0 slice-done.1
  7.0 0.0 copy-done.1
  7.0 0.0 copy-start.2
  7.1 0.0 copy-start.3
  7.1 3.1 %prepare.1 = (bf16[256,2048]{1,0:T(8,128)(2,1)S(1)}, bf16[1024,256]{1,0:T(8,128)(2,1)S(1)}, bf16[512,256]{1,0:T(8,128)(2,1)S(1)}, bf16[256,1024]{1,0:T(8,128)(2,...) custom-call(s32[1]{0:T(128)S(6)} %copy.14.step_ref, s32[32]{0:T(128)} %back_hbm.1, ...), custom_call_target="tpu_custom_call" | custom-call | flops 1610612736 | bytes 8388608 | tf_op jit(solution)/shard_map/prepare/pallas_call | solution.py:255
  10.2 0.4 collective-permute-done.partner_ref
  10.6 0.0 copy-done.2
  10.6 0.0 copy-done.3
  10.6 0.1 far.1
  10.7 0.0 copy-start
  10.7 9.1 %collective-permute-start.1 = (bf16[160,128]{1,0:T(8,128)(2,1)S(1)}, bf16[160,128]{1,0:T(8,128)(2,1)S(1)}, u32[]{:S(2)}, u32[]{:S(2)}) collective-permute-start(bf16[160,128]{1,0:T(8,128)(2,1)S(1)} %far.1), channel_id=1, source_target_pairs={{2,5},{3,4},{4,3},{5,2},{6,9},{7,8},{8,7},{9,6},{10,13},{11,12},{1... | collective-permute-start | bytes 122888 | tf_op jit(solution)/shard_map/ppermute | solution.py:826
  19.8 0.2 combine.1
  20.0 0.1 collective-permute-start.2
  20.1 0.0 copy-done
  20.1 14.3 %layer.1 = (f32[80,256]{1,0:T(8,128)}, bf16[512,1024]{1,0:T(8,128)(2,1)S(1)}, bf16[1024,512]{1,0:T(8,128)(2,1)S(1)}, bf16[512,2048]{1,0:T(8,128)(2,1)S(1)}, bf16...) custom-call(f32[80,256]{1,0:T(8,128)S(1)} %get-tuple-element.29.share_re, ...), custom_call_target="tpu_custom_call" | custom-call | flops 5000000000 | bytes 6000000 | tf_op jit(solution)/shard_map/layer/pallas_call | solution.py:580
  34.4 0.0 collective-permute-done.2.cross_ref
  34.4 0.0 collective-permute-done.1.far_ref
  34.4 13.0 %close.1 = bf16[512,1024]{1,0:T(8,128)(2,1)} custom-call(bf16[160,128]{1,0:T(8,128)(2,1)S(1)} %collective-permute-done.1.far_ref, bf16[80,128]{1,0:T(8,128)(2,1)S(1)} %collective-permute-done.2.cross_ref, f32[80,1024]{1,0:T(8,128)S(1)} %copy-done.2, bf16[256,2048]{1,0:T(8,128)(2,1)S(1)} %get-tuple-element.31.mixed_ref, ...), custom_call_target="tpu_custom_call" | custom-call | flops 2000000000 | bytes 6000000 | tf_op jit(solution)/shard_map/close/pallas_call | solution.py:746
  (1 shorter events, 0.0 us)
Async XLA Ops:
  0.6 6.4 %slice-start = ((s8[6291456]{0:T(1024)(128)(4,1)}), s8[4194304]{0:T(1024)(128)(4,1)S(1)}, s32[]{:S(2)}) async-start(s8[6291456]{0:T(1024)(128)(4,1)} %bitcast.1), calls=%async_computation | async-start | bytes 8388608
  0.6 6.4 %slice-start.1 = ((s8[6291456]{0:T(1024)(128)(4,1)}), s8[2097152]{0:T(1024)(128)(4,1)S(1)}, s32[]{:S(2)}) async-start(s8[6291456]{0:T(1024)(128)(4,1)} %bitcast.1), calls=%async_computation.1 | async-start | bytes 4194304
  0.7 6.4 %copy-start.1 = (bf16[256,3072]{1,0:T(8,128)(2,1)S(1)}, bf16[256,3072]{1,0:T(8,128)(2,1)}, u32[]{:S(2)}) copy-start(bf16[256,3072]{1,0:T(8,128)(2,1)} %time_w_ref.1) | copy-start | bytes 4718596
  3.0 7.6 %collective-permute-start = (bf16[80,512]{1,0:T(8,128)(2,1)S(1)}, bf16[80,512]{1,0:T(8,128)(2,1)S(1)}, u32[]{:S(2)}, u32[]{:S(2)}) collective-permute-start(bf16[80,512]{1,0:T(8,128)(2,1)S(1)} %get-tuple-element.28), channel_id=1, source_target_pairs={{0,1},{1,0},{2,3},{3,2},{4,5},{5,4},{6,7},{7,6},{8,9},{9,8},{10,11... | collective-permute-start | bytes 245768 | tf_op jit(solution)/shard_map/ppermute | solution.py:814
  7.0 3.5 %copy-start.2 = (f32[80,1024]{1,0:T(8,128)S(1)}, f32[80,1024]{1,0:T(8,128)}, u32[]{:S(2)}) copy-start(f32[80,1024]{1,0:T(8,128)} %prompt_ref.5) | copy-start | bytes 983044
  7.1 3.5 %copy-start.3 = (f32[80,1024]{1,0:T(8,128)S(1)}, f32[80,1024]{1,0:T(8,128)}, u32[]{:S(2)}) copy-start(f32[80,1024]{1,0:T(8,128)} %latent_ref.3) | copy-start | bytes 983044
  10.7 9.4 %copy-start = (bf16[1024,1024]{1,0:T(8,128)(2,1)S(1)}, bf16[1024,1024]{1,0:T(8,128)(2,1)}, u32[]{:S(2)}) copy-start(bf16[1024,1024]{1,0:T(8,128)(2,1)} %out_w_ref.3) | copy-start | bytes 6291460
  10.7 23.8 %collective-permute-start.1 = (bf16[160,128]{1,0:T(8,128)(2,1)S(1)}, bf16[160,128]{1,0:T(8,128)(2,1)S(1)}, u32[]{:S(2)}, u32[]{:S(2)}) collective-permute-start(bf16[160,128]{1,0:T(8,128)(2,1)S(1)} %far.1), channel_id=1, source_target_pairs={{2,5},{3,4},{4,3},{5,2},{6,9},{7,8},{8,7},{9,6},{10,13},{11,12},{1... | collective-permute-start | bytes 122888 | tf_op jit(solution)/shard_map/ppermute | solution.py:826
  20.0 14.4 %collective-permute-start.2 = (bf16[80,128]{1,0:T(8,128)(2,1)S(1)}, bf16[80,128]{1,0:T(8,128)(2,1)S(1)}, u32[]{:S(2)}, u32[]{:S(2)}) collective-permute-start(bf16[80,128]{1,0:T(8,128)(2,1)S(1)} %get-tuple-element.38), channel_id=1, source_target_pairs={{0,3},{1,2},{2,1},{3,0},{4,7},{5,6},{6,5},{7,4},{8,11},{9,10},{10,... | collective-permute-start | bytes 61448 | tf_op jit(solution)/shard_map/ppermute | solution.py:828

commit v6 on v5

--- a/solution.py
+++ b/solution.py
@@ -394,7 +394,7 @@
 
 def split_values(values, start, value_ref):
     left = lax.broadcasted_iota(jnp.int32, (values.shape[0], 128), 1) < 64
-    for part in range(2):
+    for part in range(values.shape[1] // 128):
         pair = values[:, 128 * part : 128 * (part + 1)]
         at = 2 * start + 256 * part
         value_ref[:, at : at + 128] = jnp.where(left, pair, 0.0).astype(BF16)
@@ -645,11 +645,11 @@
     after = jnp.where(half == 0, cross_rows, seq_rows).astype(BF16)
     normed = normalised(jnp.concatenate([before, after], axis=1), gram_ref, mel)
     turned = normed.T
-    for start in range(0, width, 256):
-        cols = slice(start, start + 256)
+    for start in range(0, width, 512):
+        cols = slice(start, start + 512)
         near_key_ref[cols] = mm(keyed_ref[cols], normed).astype(BF16)
         split_values(
-            mm(turned, mixed_ref[:, width + start : width + start + 256]), start, near_value_ref
+            mm(turned, mixed_ref[:, width + start : width + start + 512]), start, near_value_ref
         )
 
     edges = edges_of(frames)

time: 47.6 us -> 47.6 us (level)
  no operation moved by 1% of the time
where the time goes in v6:
time: 47.6 us; the launch traced here: 47.4 us
  Pallas kernels  33 us (69%)
  starting transfers between devices  12.6 us (26%)
  between operations  1.43 us (3%)
    pallas_call x1, Pallas kernels, layer_call(): pl.pallas_call(functools.partial(layer_kernel, mel), in_specs=[whole()] *...  14.3 us
    pallas_call x1, Pallas kernels, close_call(): pl.pallas_call(close_kernel, in_specs=[whole()] * 16, out_specs=whole(plt...  13 us
    ppermute x1, starting transfers between devices, body(): far = lax.ppermute(far, axes, to_span)  9.14 us
    ppermute x1, starting transfers between devices, body(): partner = lax.ppermute(sent, axes, to_partner)  3.36 us
    pallas_call x1, Pallas kernels, prepare_call(): pl.pallas_call(functools.partial(prepare_kernel, total_blocks), in_specs=...  3.11 us
    pallas_call x1, Pallas kernels, velocity_call(): pl.pallas_call(velocity_kernel, in_specs=[whole(pltpu.HBM)] * 2, out_spec...  2.32 us
  transfers between devices with their start and end apart: 3, of which 1 were waited for; matrix products, arithmetic and copies ran while one was open for 0% of the time, Pallas kernels for 37%

profile of v6, /device:TPU:6, one launch (start us, length us, event | category | flops | bytes accessed | tf_op | source)
XLA Modules:
  0.0 47.4 jit_solution(13153928747600770360)
XLA Ops:
  0.6 0.0 slice-start
  0.6 0.0 slice-start.1
  0.7 0.0 copy-start.1
  0.7 2.3 %velocity.1 = (f32[80,512]{1,0:T(8,128)S(1)}, bf16[80,512]{1,0:T(8,128)(2,1)S(1)}) custom-call(bf16[512,1024]{1,0:T(8,128)(2,1)} %hidden_ref.1, bf16[80,1024]{1,0:T(8,128)(2,1)} %bitcast.3), custom_call_target="tpu_custom_call" | custom-call | flops 10000000000 | bytes 1048576 | tf_op jit(solution)/shard_map/velocity/pallas_call | solution.py:119
  3.0 3.4 %collective-permute-start = (bf16[80,512]{1,0:T(8,128)(2,1)S(1)}, bf16[80,512]{1,0:T(8,128)(2,1)S(1)}, u32[]{:S(2)}, u32[]{:S(2)}) collective-permute-start(bf16[80,512]{1,0:T(8,128)(2,1)S(1)} %get-tuple-element.28), channel_id=1, source_target_pairs={{0,1},{1,0},{2,3},{3,2},{4,5},{5,4},{6,7},{7,6},{8,9},{9,8},{10,11... | collective-permute-start | bytes 245768 | tf_op jit(solution)/shard_map/ppermute | solution.py:814
  7.0 0.0 slice-done
  7.0 0.0 slice-done.1
  7.0 0.0 copy-done.1
  7.0 0.0 copy-start.2
  7.1 0.0 copy-start.3
  7.1 3.1 %prepare.1 = (bf16[256,2048]{1,0:T(8,128)(2,1)S(1)}, bf16[1024,256]{1,0:T(8,128)(2,1)S(1)}, bf16[512,256]{1,0:T(8,128)(2,1)S(1)}, bf16[256,1024]{1,0:T(8,128)(2,...) custom-call(s32[1]{0:T(128)S(6)} %copy.14.step_ref, s32[32]{0:T(128)} %back_hbm.1, ...), custom_call_target="tpu_custom_call" | custom-call | flops 1610612736 | bytes 8388608 | tf_op jit(solution)/shard_map/prepare/pallas_call | solution.py:255
  10.2 0.4 collective-permute-done.partner_ref
  10.6 0.0 copy-done.2
  10.6 0.0 copy-done.3
  10.6 0.1 far.1
  10.7 0.0 copy-start
  10.7 9.1 %collective-permute-start.1 = (bf16[160,128]{1,0:T(8,128)(2,1)S(1)}, bf16[160,128]{1,0:T(8,128)(2,1)S(1)}, u32[]{:S(2)}, u32[]{:S(2)}) collective-permute-start(bf16[160,128]{1,0:T(8,128)(2,1)S(1)} %far.1), channel_id=1, source_target_pairs={{2,5},{3,4},{4,3},{5,2},{6,9},{7,8},{8,7},{9,6},{10,13},{11,12},{1... | collective-permute-start | bytes 122888 | tf_op jit(solution)/shard_map/ppermute | solution.py:826
  19.8 0.2 combine.1
  20.0 0.1 collective-permute-start.2
  20.1 0.0 copy-done
  20.1 14.3 %layer.1 = (f32[80,256]{1,0:T(8,128)}, bf16[512,1024]{1,0:T(8,128)(2,1)S(1)}, bf16[1024,512]{1,0:T(8,128)(2,1)S(1)}, bf16[512,2048]{1,0:T(8,128)(2,1)S(1)}, bf16...) custom-call(f32[80,256]{1,0:T(8,128)S(1)} %get-tuple-element.29.share_re, ...), custom_call_target="tpu_custom_call" | custom-call | flops 5000000000 | bytes 6000000 | tf_op jit(solution)/shard_map/layer/pallas_call | solution.py:580
  34.4 0.0 collective-permute-done.2.cross_ref
  34.4 0.0 collective-permute-done.1.far_ref
  34.4 13.0 %close.1 = bf16[512,1024]{1,0:T(8,128)(2,1)} custom-call(bf16[160,128]{1,0:T(8,128)(2,1)S(1)} %collective-permute-done.1.far_ref, bf16[80,128]{1,0:T(8,128)(2,1)S(1)} %collective-permute-done.2.cross_ref, f32[80,1024]{1,0:T(8,128)S(1)} %copy-done.2, bf16[256,2048]{1,0:T(8,128)(2,1)S(1)} %get-tuple-element.31.mixed_ref, ...), custom_call_target="tpu_custom_call" | custom-call | flops 2000000000 | bytes 6000000 | tf_op jit(solution)/shard_map/close/pallas_call | solution.py:746
  (1 shorter events, 0.0 us)
Async XLA Ops:
  0.6 6.4 %slice-start = ((s8[6291456]{0:T(1024)(128)(4,1)}), s8[4194304]{0:T(1024)(128)(4,1)S(1)}, s32[]{:S(2)}) async-start(s8[6291456]{0:T(1024)(128)(4,1)} %bitcast.1), calls=%async_computation | async-start | bytes 8388608
  0.6 6.4 %slice-start.1 = ((s8[6291456]{0:T(1024)(128)(4,1)}), s8[2097152]{0:T(1024)(128)(4,1)S(1)}, s32[]{:S(2)}) async-start(s8[6291456]{0:T(1024)(128)(4,1)} %bitcast.1), calls=%async_computation.1 | async-start | bytes 4194304
  0.7 6.4 %copy-start.1 = (bf16[256,3072]{1,0:T(8,128)(2,1)S(1)}, bf16[256,3072]{1,0:T(8,128)(2,1)}, u32[]{:S(2)}) copy-start(bf16[256,3072]{1,0:T(8,128)(2,1)} %time_w_ref.1) | copy-start | bytes 4718596
  3.0 7.6 %collective-permute-start = (bf16[80,512]{1,0:T(8,128)(2,1)S(1)}, bf16[80,512]{1,0:T(8,128)(2,1)S(1)}, u32[]{:S(2)}, u32[]{:S(2)}) collective-permute-start(bf16[80,512]{1,0:T(8,128)(2,1)S(1)} %get-tuple-element.28), channel_id=1, source_target_pairs={{0,1},{1,0},{2,3},{3,2},{4,5},{5,4},{6,7},{7,6},{8,9},{9,8},{10,11... | collective-permute-start | bytes 245768 | tf_op jit(solution)/shard_map/ppermute | solution.py:814
  7.0 3.5 %copy-start.2 = (f32[80,1024]{1,0:T(8,128)S(1)}, f32[80,1024]{1,0:T(8,128)}, u32[]{:S(2)}) copy-start(f32[80,1024]{1,0:T(8,128)} %prompt_ref.5) | copy-start | bytes 983044
  7.1 3.5 %copy-start.3 = (f32[80,1024]{1,0:T(8,128)S(1)}, f32[80,1024]{1,0:T(8,128)}, u32[]{:S(2)}) copy-start(f32[80,1024]{1,0:T(8,128)} %latent_ref.3) | copy-start | bytes 983044
  10.7 9.4 %copy-start = (bf16[1024,1024]{1,0:T(8,128)(2,1)S(1)}, bf16[1024,1024]{1,0:T(8,128)(2,1)}, u32[]{:S(2)}) copy-start(bf16[1024,1024]{1,0:T(8,128)(2,1)} %out_w_ref.3) | copy-start | bytes 6291460
  10.7 23.8 %collective-permute-start.1 = (bf16[160,128]{1,0:T(8,128)(2,1)S(1)}, bf16[160,128]{1,0:T(8,128)(2,1)S(1)}, u32[]{:S(2)}, u32[]{:S(2)}) collective-permute-start(bf16[160,128]{1,0:T(8,128)(2,1)S(1)} %far.1), channel_id=1, source_target_pairs={{2,5},{3,4},{4,3},{5,2},{6,9},{7,8},{8,7},{9,6},{10,13},{11,12},{1... | collective-permute-start | bytes 122888 | tf_op jit(solution)/shard_map/ppermute | solution.py:826
  20.0 14.4 %collective-permute-start.2 = (bf16[80,128]{1,0:T(8,128)(2,1)S(1)}, bf16[80,128]{1,0:T(8,128)(2,1)S(1)}, u32[]{:S(2)}, u32[]{:S(2)}) collective-permute-start(bf16[80,128]{1,0:T(8,128)(2,1)S(1)} %get-tuple-element.38), channel_id=1, source_target_pairs={{0,3},{1,2},{2,1},{3,0},{4,7},{5,6},{6,5},{7,4},{8,11},{9,10},{10,... | collective-permute-start | bytes 61448 | tf_op jit(solution)/shard_map/ppermute | solution.py:828
